TPU v7x, 512 devices: a whole 4x4x16 slice. The times are simulated.
512 devices in a mesh: row: 16 (over x_hi, y, core), col: 32 (over z, x_lo).
Axes of the slice: x: 4 (x_hi: 2, x_lo: 2; x = x_hi * 2 + x_lo), y: 4, z: 16, core: 2. Of those that a mesh axis runs over, the one named last changes fastest.
Arguments:
- coefficients: bfloat16 [32, 1048576], P(None, ('row', 'col')), may hold values from -6 to 6
- factors: bfloat16 [4, 16384, 128, 64], P(None, ('row', 'col')), may hold values from -0.5 to 0.5
- pattern: int32 [4, 16384], P(None, ('row', 'col')), may hold values from 0 to 31, as said below
- octree_order: int32 [16384], P(('row', 'col')), may hold values from 0 to 31, as said below
- panels: bfloat16 [32, 1048576], P(None, ('row', 'col')), may hold values from -6 to 6
- near_blocks: bfloat16 [16384, 6, 64, 64], P(('row', 'col')), may hold values from -0.3125 to 0.3125
- neighbors: int32 [16384, 6], P(('row', 'col')), may hold values from 0 to 16383, as said below
Outputs:
- far_field: bfloat16 [32, 1048576], P(None, ('row', 'col'))
- near_field: bfloat16 [32, 1048576], P(None, ('row', 'col'))
Inputs may be any that keep to these rules, and one draw needn't show every extreme that they name: `pattern`: for every level, the entries of one device's 32 boxes are a permutation of 0 .. 31. `octree_order`: the entries of one device's 32 boxes are a permutation of 0 .. 31. `neighbors`: every entry lies within 32 of its own panel number g; entry 0 is g itself; entry 1 is g + 32 or g - 32, limited to 0 .. 16383.
All inputs are finite; a program needn't handle non-finite values.
Results may differ from a plain program's by a relative error of at most 0.0064.
Values may be sent and summed in bfloat16 or wider, within the bound.
No kernel may reach another device: no remote copies, remote signals or barrier semaphores. Data moves between devices by JAX's collectives and lax.ppermute only.
A program may use at most 64 MiB of HBM per device.

v0:
```python
import jax
import jax.numpy as jnp
from jax import lax
from jax.sharding import PartitionSpec as P


def partner_2(value, axis, distance):
    mask = 2**distance
    pairs = [(source, source ^ mask) for source in range(lax.axis_size(axis))]
    return lax.ppermute(value, axis, pairs)


def padded(value, sides, width):
    for axis, dim in sides:
        size, length = (lax.axis_size(axis), value.shape[dim])
        up = [(i, (i + 1) % size) for i in range(size - 1)]
        down = [(j, i) for i, j in up]
        last = lax.slice_in_dim(value, length - width, length, axis=dim)
        leading = lax.slice_in_dim(value, 0, width, axis=dim)
        before = lax.ppermute(last, axis, up)
        after = lax.ppermute(leading, axis, down)
        value = jnp.concatenate([before, value, after], axis=dim)
    return value


def combine(blocks, partner, index, matrix):
    chosen = jnp.take(partner, index, axis=1)
    stacked = jnp.concatenate([blocks, chosen], axis=2)
    return jnp.einsum("kbi,bio->kbo", stacked, matrix, preferred_element_type=jnp.float32).astype(
        jnp.bfloat16
    )


def per_device(coefficients, factors, pattern, octree_order, panels, near_blocks, neighbors):
    rhs_count = coefficients.shape[0]
    box_count = pattern.shape[1]
    rank = factors.shape[3]
    width = near_blocks.shape[2]
    blocks = coefficients.reshape(rhs_count, box_count, rank)
    col_bits = lax.axis_size("col").bit_length() - 1
    row_bits = lax.axis_size("row").bit_length() - 1
    for level in range(factors.shape[0]):
        if level % 2 == 0:
            partner = partner_2(blocks, "col", col_bits - 1 - level // 2)
        else:
            partner = partner_2(blocks, "row", row_bits - 1 - level // 2)
        blocks = combine(blocks, partner, pattern[level], factors[level])
    far_field = jnp.take(blocks, octree_order, axis=1).reshape(rhs_count, box_count * rank)
    extended = padded(panels, ((("row", "col"), 1),), box_count * width)
    extended = extended.reshape(rhs_count, 3 * box_count, width)
    first_box = lax.axis_index(("row", "col")) * box_count - box_count
    local_index = neighbors - first_box
    taken = jnp.take(extended, local_index, axis=1)
    near_sum = jnp.einsum("kbnp,bnpq->kbq", taken, near_blocks, preferred_element_type=jnp.float32)
    near_field = near_sum.astype(jnp.bfloat16).reshape(rhs_count, box_count * width)
    return (far_field, near_field)


def solution(mesh):
    in_specs = (
        P(None, ("row", "col")),
        P(None, ("row", "col"), None, None),
        P(None, ("row", "col")),
        P(("row", "col")),
        P(None, ("row", "col")),
        P(("row", "col"), None, None, None),
        P(("row", "col"), None),
    )
    out_specs = (P(None, ("row", "col")), P(None, ("row", "col")))
    return jax.shard_map(
        per_device, mesh=mesh, in_specs=in_specs, out_specs=out_specs, check_vma=False
    )
```

profile of v0, /device:TPU:24, one launch (start us, length us, event | category | flops | bytes accessed | tf_op | source)
XLA Modules:
  0.0 117.4 jit_solution(14497546970699928181)
XLA Ops:
  0.6 3.7 %collective-permute-start.4 = (bf16[32,2048]{1,0:T(8,128)(2,1)}, bf16[32,2048]{1,0:T(8,128)(2,1)S(1)}, u32[]{:S(2)}, u32[]{:S(2)}) collective-permute-start(bf16[32,2048]{1,0:T(8,128)(2,1)} %param.13), channel_id=1, source_target_pairs={{0,1},{1,2},{2,3},{3,4},{4,5},{5,6},{6,7},{7,8},{8,9},{9,10},{10,1... | collective-permute-start | bytes 393224 | tf_op jit(solution)/shard_map/ppermute | solution.py:20
  4.3 10.5 %collective-permute-start.5 = (bf16[32,2048]{1,0:T(8,128)(2,1)}, bf16[32,2048]{1,0:T(8,128)(2,1)}, u32[]{:S(2)}, u32[]{:S(2)}) collective-permute-start(bf16[32,2048]{1,0:T(8,128)(2,1)} %param.13), channel_id=1, source_target_pairs={{1,0},{2,1},{3,2},{4,3},{5,4},{6,5},{7,6},{8,7},{9,8},{10,9},{11,1... | collective-permute-start | bytes 393224 | tf_op jit(solution)/shard_map/ppermute | solution.py:21
  14.8 1.9 %reshape.26 = bf16[32,32,64]{2,1,0:T(8,128)(2,1)} reshape(bf16[32,2048]{1,0:T(8,128)(2,1)} %param.9) | data formatting | bytes 262144 | tf_op jit(solution)/shard_map/reshape | solution.py:39
  16.7 1.1 copy.18
  17.8 9.8 %collective-permute-start = (bf16[32,32,64]{2,0,1:T(8,128)(2,1)S(1)}, bf16[32,32,64]{2,0,1:T(8,128)(2,1)}, u32[]{:S(2)}, u32[]{:S(2)}) collective-permute-start(bf16[32,32,64]{2,0,1:T(8,128)(2,1)S(1)} %copy.18), channel_id=1, source_target_pairs={{0,16},{1,17},{2,18},{3,19},{4,20},{5,21},{6,22},{7,23},{8,24},{9,... | collective-permute-start | bytes 393224 | tf_op jit(solution)/shard_map/ppermute | solution.py:10
  27.6 1.1 compare_select_fusion.1
  28.7 1.2 %compare_and_fusion.1 = pred[32]{0:T(512)(128)(4,1)} fusion(s32[32]{0:T(128)} %param.12), kind=kLoop, calls=%fused_computation.61 | loop fusion | flops 192 | bytes 160 | tf_op jit(solution)/shard_map/jit(_take)/and | solution.py:48
  29.9 1.4 %compare_and_fusion.2 = (pred[32]{0:T(512)(128)(4,1)}, s32[32]{0:T(128)S(1)}, pred[32]{0:T(512)(128)(4,1)}, s32[32]{0:T(128)S(1)}, pred[32]{0:T(512)(128)(4,1)S(...) fusion(s32[4,32]{1,0:T(4,128)} %param.11), kind=kLoop, calls=%fused_computation.62 | loop fusion | flops 768 | bytes 1152 | tf_op jit(solution)/shard_map/jit(_take)/and | solution.py:27
  31.9 1.3 %compare_and_fusion = (pred[32,6]{0,1:T(8,128)(4,1)}, s32[32,6]{0,1:T(8,128)}) fusion(s32[32,6]{0,1:T(8,128)} %param.15, s32[]{:T(128)S(6)} %sub.9), kind=kLoop, calls=%fused_computation.55 | loop fusion | flops 1344 | bytes 1732 | tf_op jit(solution)/shard_map/jit(_take)/and | solution.py:53
  34.4 19.5 %collective-permute-done = bf16[32,32,64]{2,0,1:T(8,128)(2,1)} collective-permute-done((bf16[32,32,64]{2,0,1:T(8,128)(2,1)S(1)}, bf16[32,32,64]{2,0,1:T(8,128)(2,1)}, u32[]{:S(2)}, u32[]{:S(2)}) %collective-permute-start) | collective-permute-done | bytes 131104 | tf_op jit(solution)/shard_map/ppermute | solution.py:10
  53.9 2.2 %gather_fusion.1 = bf16[32,32,64]{2,1,0:T(8,128)(2,1)} fusion(bf16[32,32,64]{2,0,1:T(8,128)(2,1)} %collective-permute-done, s32[1024]{0:T(1024)S(1)} %pad_clamp_fusion.5), kind=kCustom, calls=%fused_computation.clone | custom fusion | bytes 262272 | tf_op jit(solution)/shard_map/jit(_take)/gather | solution.py:27
  57.2 1.6 %fusion.10 = bf16[32,32,64]{2,0,1:T(8,128)(2,1)S(1)} fusion(bf16[4,32,128,64]{2,3,1,0:T(8,128)(2,1)} %param.10, bf16[32,32,64]{2,0,1:T(8,128)(2,1)S(1)} %select_bitcast_fusion.4, bf16[32,32,64]{2,0,1:T(8,128)(2,1)} %copy-done.1), kind=kOutput, calls=%fused_computation.16 | convolution fusion | flops 17367040 | bytes 1048576 | tf_op jit(solution)/shard_map/kbi,bio->kbo/dot_general | solution.py:29
  58.7 4.6 %collective-permute-start.1 = (bf16[32,32,64]{2,0,1:T(8,128)(2,1)S(1)}, bf16[32,32,64]{2,0,1:T(8,128)(2,1)}, u32[]{:S(2)}, u32[]{:S(2)}) collective-permute-start(bf16[32,32,64]{2,0,1:T(8,128)(2,1)S(1)} %fusion.10), channel_id=1, source_target_pairs={{0,256},{32,288},{64,320},{96,352},{128,384},{160,416},{192,448},{... | collective-permute-start | bytes 393224 | tf_op jit(solution)/shard_map/ppermute | solution.py:10
  66.9 3.3 %collective-permute-done.1 = bf16[32,32,64]{2,0,1:T(8,128)(2,1)} collective-permute-done((bf16[32,32,64]{2,0,1:T(8,128)(2,1)S(1)}, bf16[32,32,64]{2,0,1:T(8,128)(2,1)}, u32[]{:S(2)}, u32[]{:S(2)}) %collective-permute-start.1) | collective-permute-done | bytes 131104 | tf_op jit(solution)/shard_map/ppermute | solution.py:10
  70.2 2.4 %gather_fusion.2 = bf16[32,32,64]{2,1,0:T(8,128)(2,1)} fusion(bf16[32,32,64]{2,0,1:T(8,128)(2,1)} %collective-permute-done.1, s32[1024]{0:T(1024)} %pad_clamp_fusion.4), kind=kCustom, calls=%fused_computation.1.clone | custom fusion | bytes 262272 | tf_op jit(solution)/shard_map/jit(_take)/gather | solution.py:27
  72.5 1.1 select_bitcast_fusion.3
  73.6 2.2 %fusion.11 = bf16[32,32,64]{2,0,1:T(8,128)(2,1)} fusion(bf16[4,32,128,64]{2,3,1,0:T(8,128)(2,1)} %param.10, bf16[32,32,64]{2,0,1:T(8,128)(2,1)S(1)} %select_bitcast_fusion.3, bf16[32,32,64]{2,0,1:T(8,128)(2,1)S(1)} %fusion.10), kind=kOutput, calls=%fused_computation.17 | convolution fusion | flops 17367040 | bytes 917504 | tf_op jit(solution)/shard_map/kbi,bio->kbo/dot_general | solution.py:29
  75.8 1.9 %collective-permute-start.2 = (bf16[32,32,64]{2,0,1:T(8,128)(2,1)}, bf16[32,32,64]{2,0,1:T(8,128)(2,1)}, u32[]{:S(2)}, u32[]{:S(2)}) collective-permute-start(bf16[32,32,64]{2,0,1:T(8,128)(2,1)} %fusion.11), channel_id=1, source_target_pairs={{0,8},{1,9},{2,10},{3,11},{4,12},{5,13},{6,14},{7,15},{8,0},{9,1},... | collective-permute-start | bytes 393224 | tf_op jit(solution)/shard_map/ppermute | solution.py:10
  78.4 1.1 pad_maximum_fusion
  79.4 1.7 %reshape.28 = bf16[32,96,64]{2,1,0:T(8,128)(2,1)} reshape(bf16[32,6144]{1,0:T(8,128)(2,1)S(1)} %pad_maximum_fusion) | data formatting | bytes 786432 | tf_op jit(solution)/shard_map/reshape | solution.py:50
  81.2 2.3 %copy.22 = bf16[32,96,64]{2,0,1:T(8,128)(2,1)} copy(bf16[32,96,64]{2,1,0:T(8,128)(2,1)} %reshape.28) | data formatting | bytes 786432 | tf_op jit(solution)/shard_map/reshape | solution.py:50
  83.5 3.2 %gather_fusion = bf16[192,32,64]{2,1,0:T(8,128)(2,1)} fusion(bf16[32,96,64]{2,0,1:T(8,128)(2,1)} %copy.22, s32[1024]{0:T(1024)S(1)} %pad_clamp_fusion), kind=kCustom, calls=%fused_computation.5 | custom fusion | bytes 1573632 | tf_op jit(solution)/shard_map/jit(_take)/gather | solution.py:53
  86.6 7.2 %collective-permute-done.2 = bf16[32,32,64]{2,0,1:T(8,128)(2,1)} collective-permute-done((bf16[32,32,64]{2,0,1:T(8,128)(2,1)}, bf16[32,32,64]{2,0,1:T(8,128)(2,1)}, u32[]{:S(2)}, u32[]{:S(2)}) %collective-permute-start.2) | collective-permute-done | bytes 131104 | tf_op jit(solution)/shard_map/ppermute | solution.py:10
  93.8 1.7 %gather_fusion.3 = bf16[32,32,64]{2,1,0:T(8,128)(2,1)S(1)} fusion(bf16[32,32,64]{2,0,1:T(8,128)(2,1)} %collective-permute-done.2, s32[1024]{0:T(1024)} %pad_clamp_fusion.3), kind=kCustom, calls=%fused_computation.2.clone | custom fusion | bytes 262272 | tf_op jit(solution)/shard_map/jit(_take)/gather | solution.py:27
  95.6 1.6 %fusion.12 = bf16[32,32,64]{2,0,1:T(8,128)(2,1)S(1)} fusion(bf16[4,32,128,64]{2,3,1,0:T(8,128)(2,1)} %param.10, bf16[32,32,64]{2,0,1:T(8,128)(2,1)S(1)} %select_bitcast_fusion.2, bf16[32,32,64]{2,0,1:T(8,128)(2,1)} %fusion.11), kind=kOutput, calls=%fused_computation.18 | convolution fusion | flops 17367040 | bytes 1048576 | tf_op jit(solution)/shard_map/kbi,bio->kbo/dot_general | solution.py:29
  97.2 3.1 %collective-permute-start.3 = (bf16[32,32,64]{2,0,1:T(8,128)(2,1)S(1)}, bf16[32,32,64]{2,0,1:T(8,128)(2,1)}, u32[]{:S(2)}, u32[]{:S(2)}) collective-permute-start(bf16[32,32,64]{2,0,1:T(8,128)(2,1)S(1)} %fusion.12), channel_id=1, source_target_pairs={{0,128},{32,160},{64,192},{96,224},{128,0},{160,32},{192,64},{224,... | collective-permute-start | bytes 393224 | tf_op jit(solution)/shard_map/ppermute | solution.py:10
  100.4 2.5 %fusion.14 = bf16[32,32,64]{2,0,1:T(8,128)(2,1)S(1)} fusion(bf16[32,6,64,64]{3,2,1,0:T(8,128)(2,1)S(1)} %copy-done, bf16[32,6,32,64]{3,2,1,0:T(8,128)(2,1)} %bitcast.62, pred[32,6]{1,0:T(8,128)(4,1)S(1)} %copy.20), kind=kOutput, calls=%fused_computation.20 | convolution fusion | flops 50790400 | bytes 2490560 | tf_op jit(solution)/shard_map/kbnp,bnpq->kbq/dot_general | solution.py:54
  103.7 1.9 %reshape.29 = bf16[32,2048]{1,0:T(8,128)(2,1)} reshape(bf16[32,32,64]{2,1,0:T(8,128)(2,1)} %copy.23) | data formatting | bytes 262144 | tf_op jit(solution)/shard_map/reshape | solution.py:55
  105.6 3.3 %collective-permute-done.3 = bf16[32,32,64]{2,0,1:T(8,128)(2,1)} collective-permute-done((bf16[32,32,64]{2,0,1:T(8,128)(2,1)S(1)}, bf16[32,32,64]{2,0,1:T(8,128)(2,1)}, u32[]{:S(2)}, u32[]{:S(2)}) %collective-permute-start.3) | collective-permute-done | bytes 131104 | tf_op jit(solution)/shard_map/ppermute | solution.py:10
  108.9 2.4 %gather_fusion.4 = bf16[32,32,64]{2,1,0:T(8,128)(2,1)} fusion(bf16[32,32,64]{2,0,1:T(8,128)(2,1)} %collective-permute-done.3, s32[1024]{0:T(1024)} %pad_clamp_fusion.2), kind=kCustom, calls=%fused_computation.3.clone | custom fusion | bytes 262272 | tf_op jit(solution)/shard_map/jit(_take)/gather | solution.py:27
  112.4 2.2 %fusion.13 = bf16[32,32,64]{2,0,1:T(8,128)(2,1)} fusion(bf16[4,32,128,64]{2,3,1,0:T(8,128)(2,1)} %param.10, bf16[32,32,64]{2,0,1:T(8,128)(2,1)S(1)} %select_bitcast_fusion.1, bf16[32,32,64]{2,0,1:T(8,128)(2,1)S(1)} %fusion.12), kind=kOutput, calls=%fused_computation.19 | convolution fusion | flops 17367040 | bytes 917504 | tf_op jit(solution)/shard_map/kbi,bio->kbo/dot_general | solution.py:29
  114.6 1.7 %gather_fusion.5 = bf16[32,32,64]{2,1,0:T(8,128)(2,1)S(1)} fusion(bf16[32,32,64]{2,0,1:T(8,128)(2,1)} %fusion.13, s32[1024]{0:T(1024)} %pad_clamp_fusion.1), kind=kCustom, calls=%fused_computation.4.clone | custom fusion | bytes 262272 | tf_op jit(solution)/shard_map/jit(_take)/gather | solution.py:48
  (32 shorter events, 10.1 us)
Async XLA Ops:
  0.6 99.7 %copy-start = (bf16[32,6,64,64]{3,2,1,0:T(8,128)(2,1)S(1)}, bf16[32,6,64,64]{3,2,1,0:T(8,128)(2,1)}, u32[]{:S(2)}) copy-start(bf16[32,6,64,64]{3,2,1,0:T(8,128)(2,1)} %param.14) | copy-start | bytes 4718596
  0.6 77.1 %collective-permute-start.4 = (bf16[32,2048]{1,0:T(8,128)(2,1)}, bf16[32,2048]{1,0:T(8,128)(2,1)S(1)}, u32[]{:S(2)}, u32[]{:S(2)}) collective-permute-start(bf16[32,2048]{1,0:T(8,128)(2,1)} %param.13), channel_id=1, source_target_pairs={{0,1},{1,2},{2,3},{3,4},{4,5},{5,6},{6,7},{7,8},{8,9},{9,10},{10,1... | collective-permute-start | bytes 393224 | tf_op jit(solution)/shard_map/ppermute | solution.py:20
  4.3 74.1 %collective-permute-start.5 = (bf16[32,2048]{1,0:T(8,128)(2,1)}, bf16[32,2048]{1,0:T(8,128)(2,1)}, u32[]{:S(2)}, u32[]{:S(2)}) collective-permute-start(bf16[32,2048]{1,0:T(8,128)(2,1)} %param.13), channel_id=1, source_target_pairs={{1,0},{2,1},{3,2},{4,3},{5,4},{6,5},{7,6},{8,7},{9,8},{10,9},{11,1... | collective-permute-start | bytes 393224 | tf_op jit(solution)/shard_map/ppermute | solution.py:21
  17.7 38.4 %copy-start.1 = (bf16[32,32,64]{2,0,1:T(8,128)(2,1)}, bf16[32,32,64]{2,0,1:T(8,128)(2,1)S(1)}, u32[]{:S(2)}) copy-start(bf16[32,32,64]{2,0,1:T(8,128)(2,1)S(1)} %copy.18) | copy-start | bytes 393220
  17.8 36.1 %collective-permute-start = (bf16[32,32,64]{2,0,1:T(8,128)(2,1)S(1)}, bf16[32,32,64]{2,0,1:T(8,128)(2,1)}, u32[]{:S(2)}, u32[]{:S(2)}) collective-permute-start(bf16[32,32,64]{2,0,1:T(8,128)(2,1)S(1)} %copy.18), channel_id=1, source_target_pairs={{0,16},{1,17},{2,18},{3,19},{4,20},{5,21},{6,22},{7,23},{8,24},{9,... | collective-permute-start | bytes 393224 | tf_op jit(solution)/shard_map/ppermute | solution.py:10
  33.8 29.6 %copy-start.6 = (s32[32]{0:T(128)S(1)}, s32[32]{0:T(128)}, u32[]{:S(2)}) copy-start(s32[32]{0:T(128)} %compare_select_fusion.1) | copy-start | bytes 388
  58.7 11.4 %collective-permute-start.1 = (bf16[32,32,64]{2,0,1:T(8,128)(2,1)S(1)}, bf16[32,32,64]{2,0,1:T(8,128)(2,1)}, u32[]{:S(2)}, u32[]{:S(2)}) collective-permute-start(bf16[32,32,64]{2,0,1:T(8,128)(2,1)S(1)} %fusion.10), channel_id=1, source_target_pairs={{0,256},{32,288},{64,320},{96,352},{128,384},{160,416},{192,448},{... | collective-permute-start | bytes 393224 | tf_op jit(solution)/shard_map/ppermute | solution.py:10
  75.8 18.0 %collective-permute-start.2 = (bf16[32,32,64]{2,0,1:T(8,128)(2,1)}, bf16[32,32,64]{2,0,1:T(8,128)(2,1)}, u32[]{:S(2)}, u32[]{:S(2)}) collective-permute-start(bf16[32,32,64]{2,0,1:T(8,128)(2,1)} %fusion.11), channel_id=1, source_target_pairs={{0,8},{1,9},{2,10},{3,11},{4,12},{5,13},{6,14},{7,15},{8,0},{9,1},... | collective-permute-start | bytes 393224 | tf_op jit(solution)/shard_map/ppermute | solution.py:10
  77.7 0.7 copy-start.2
  83.5 12.0 %copy-start.4 = (pred[32]{0:T(512)(128)(4,1)S(1)}, pred[32]{0:T(512)(128)(4,1)}, u32[]{:S(2)}) copy-start(pred[32]{0:T(512)(128)(4,1)} %get-tuple-element.17) | copy-start | bytes 100
  97.2 11.7 %collective-permute-start.3 = (bf16[32,32,64]{2,0,1:T(8,128)(2,1)S(1)}, bf16[32,32,64]{2,0,1:T(8,128)(2,1)}, u32[]{:S(2)}, u32[]{:S(2)}) collective-permute-start(bf16[32,32,64]{2,0,1:T(8,128)(2,1)S(1)} %fusion.12), channel_id=1, source_target_pairs={{0,128},{32,160},{64,192},{96,224},{128,0},{160,32},{192,64},{224,... | collective-permute-start | bytes 393224 | tf_op jit(solution)/shard_map/ppermute | solution.py:10
  100.4 10.9 %copy-start.3 = (pred[32]{0:T(512)(128)(4,1)S(1)}, pred[32]{0:T(512)(128)(4,1)}, u32[]{:S(2)}) copy-start(pred[32]{0:T(512)(128)(4,1)} %get-tuple-element.5) | copy-start | bytes 100
  102.9 13.3 %copy-start.5 = (pred[32]{0:T(512)(128)(4,1)S(1)}, pred[32]{0:T(512)(128)(4,1)}, u32[]{:S(2)}) copy-start(pred[32]{0:T(512)(128)(4,1)} %compare_and_fusion.1) | copy-start | bytes 100
where the time goes:
time: 119 us; the launch traced here: 117 us
  starting transfers between devices  33.6 us (28%)
  waiting for transfers between devices  33.3 us (28%)
  local copies, waits for them, and re-layouts  27 us (23%)
  other arithmetic  12.5 us (11%)
  matrix products  10 us (8%)
    ppermute x4, waiting for transfers between devices, partner_2(): return lax.ppermute(value, axis, pairs)  33.3 us
    ppermute x4, starting transfers between devices, partner_2(): return lax.ppermute(value, axis, pairs)  19.5 us
    ppermute x1, starting transfers between devices, padded(): after = lax.ppermute(leading, axis, down)  10.5 us
    gather x4, local copies, waits for them, and re-layouts, combine(): chosen = jnp.take(partner, index, axis=1)  8.64 us
    dot_general x4, matrix products, combine(): jnp.einsum('kbi,bio->kbo', stacked, matrix, preferred_element_type=jnp.fl...  7.53 us
    reshape x2, local copies, waits for them, and re-layouts, per_device(): extended = extended.reshape(rhs_count, 3 * box_count, width)  4.03 us
    ppermute x1, starting transfers between devices, padded(): before = lax.ppermute(last, axis, up)  3.66 us
    select_n x4, other arithmetic, combine(): chosen = jnp.take(partner, index, axis=1)  3.26 us
  transfers between devices with their start and end apart: 6, of which 4 were waited for; matrix products, arithmetic and copies ran while one was open for 32% of the time, Pallas kernels for 0%

commit v1 on v0

v1 whole, which is shorter than its diff:
```python
import functools

import jax
import jax.numpy as jnp
from jax import lax
from jax.experimental import pallas as pl
from jax.experimental.pallas import tpu as pltpu
from jax.sharding import PartitionSpec as P

LANES = 128
NT = (((1,), (1,)), ((), ()))


def exchange(value, axis, mask):
    pairs = [(i, i ^ mask) for i in range(lax.axis_size(axis))]
    return lax.ppermute(value, axis, pairs)


def tile_of(ref, box):
    start = pl.multiple_of((box >> 1) * LANES, LANES)
    return ref[:, pl.ds(start, LANES)]


def placed(tile, box, upper):
    half = box & 1
    shift = (1 - half if upper else half) * (LANES // 2)
    return pltpu.roll(tile, shift, 1)


def level_body(level, ordered, pattern, order, own, partner, matrices, out):
    rows = own.shape[0]
    boxes = matrices.shape[0]
    low = lax.broadcasted_iota(jnp.int32, (rows, LANES), 1) < LANES // 2
    for pair in range(boxes // 2):
        sides = []
        weights = []
        for g in (2 * pair, 2 * pair + 1):
            box = order[g] if ordered else g
            if ordered:
                mine = placed(tile_of(own, box), box, False)
            else:
                mine = own[:, pair * LANES : (pair + 1) * LANES]
                if g & 1:
                    mine = pltpu.roll(mine, LANES // 2, 1)
            q = pattern[level, box]
            theirs = placed(tile_of(partner, q), q, True)
            sides.append(jnp.where(low, mine, theirs))
            weights.append(matrices[box])
        product = lax.dot_general(
            jnp.concatenate(sides, axis=0),
            jnp.concatenate(weights, axis=0),
            NT,
            preferred_element_type=jnp.float32,
        )
        joined = jnp.where(low, product[:rows], product[rows:])
        out[:, pair * LANES : (pair + 1) * LANES] = joined.astype(out.dtype)


def combine(level, ordered, pattern, order, own, partner, matrices):
    _, boxes, rank, depth = matrices.shape
    smem = pl.BlockSpec(memory_space=pltpu.SMEM)
    vmem = pl.BlockSpec(memory_space=pltpu.VMEM)
    return pl.pallas_call(
        functools.partial(level_body, level, ordered),
        grid=(1,),
        out_shape=jax.ShapeDtypeStruct(own.shape, own.dtype),
        in_specs=[
            smem,
            smem,
            vmem,
            vmem,
            pl.BlockSpec((None, boxes, rank, depth), lambda i: (level, 0, 0, 0)),
        ],
        out_specs=vmem,
        cost_estimate=pl.CostEstimate(
            flops=2 * own.size * depth, bytes_accessed=1 << 20, transcendentals=0
        ),
        name=f"level{level}",
    )(pattern, order, own, partner, matrices)


def near_body(first, neighbors, before, own, after, matrices, out, held):
    rows = own.shape[0]
    boxes, near, width, _ = matrices.shape
    tiles = own.shape[1] // LANES
    for part, source in enumerate((before, own, after)):
        for t in range(tiles):
            tile = source[:, t * LANES : (t + 1) * LANES]
            held[0, part * tiles + t] = tile
            held[1, part * tiles + t] = pltpu.roll(tile, LANES // 2, 1)
    low = lax.broadcasted_iota(jnp.int32, (rows, LANES), 1) < LANES // 2
    base = first[0]
    for pair in range(boxes // 2):
        sums = []
        for g in (2 * pair, 2 * pair + 1):
            sides = []
            for n in range(0, near, 2):
                a = neighbors[n, g] - base
                b = neighbors[n + 1, g] - base
                lower = held[a & 1, a >> 1]
                upper = held[1 - (b & 1), b >> 1]
                sides.append(jnp.where(low, lower, upper))
            sums.append(
                jnp.dot(
                    jnp.concatenate(sides, axis=1),
                    matrices[g].reshape(near * width, width),
                    preferred_element_type=jnp.float32,
                )
            )
        joined = jnp.concatenate(sums, axis=1).astype(out.dtype)
        out[:, pair * LANES : (pair + 1) * LANES] = joined


def near_sums(first, neighbors, before, own, after, matrices):
    smem = pl.BlockSpec(memory_space=pltpu.SMEM)
    vmem = pl.BlockSpec(memory_space=pltpu.VMEM)
    rows, columns = own.shape
    return pl.pallas_call(
        near_body,
        out_shape=jax.ShapeDtypeStruct(own.shape, own.dtype),
        in_specs=[smem, smem, vmem, vmem, vmem, vmem],
        out_specs=vmem,
        scratch_shapes=[pltpu.VMEM((2, 3 * columns // LANES, rows, LANES), own.dtype)],
        cost_estimate=pl.CostEstimate(
            flops=2 * own.size * 384, bytes_accessed=4 << 20, transcendentals=0
        ),
        name="near",
    )(first, neighbors, before, own, after, matrices)


def per_device(coefficients, factors, pattern, octree_order, panels, near_blocks, neighbors):
    boxes = pattern.shape[1]
    col_bits = lax.axis_size("col").bit_length() - 1
    row_bits = lax.axis_size("row").bit_length() - 1
    matrices = jnp.swapaxes(factors, 2, 3)
    blocks = coefficients
    levels = factors.shape[0]
    for level in range(levels):
        if level % 2 == 0:
            partner = exchange(blocks, "col", 1 << (col_bits - 1 - level // 2))
        else:
            partner = exchange(blocks, "row", 1 << (row_bits - 1 - level // 2))
        blocks = combine(
            level, level == levels - 1, pattern, octree_order, blocks, partner, matrices
        )
    both = ("row", "col")
    count = lax.axis_size(both)
    up = [(i, i + 1) for i in range(count - 1)]
    down = [(j, i) for i, j in up]
    before = lax.ppermute(panels, both, up)
    after = lax.ppermute(panels, both, down)
    first = (lax.axis_index(both) * boxes - boxes).astype(jnp.int32).reshape(1)
    near_field = near_sums(
        first, jnp.swapaxes(neighbors, 0, 1), before, panels, after, near_blocks
    )
    return (blocks, near_field)


def solution(mesh):
    in_specs = (
        P(None, ("row", "col")),
        P(None, ("row", "col"), None, None),
        P(None, ("row", "col")),
        P(("row", "col")),
        P(None, ("row", "col")),
        P(("row", "col"), None, None, None),
        P(("row", "col"), None),
    )
    out_specs = (P(None, ("row", "col")), P(None, ("row", "col")))
    return jax.shard_map(
        per_device, mesh=mesh, in_specs=in_specs, out_specs=out_specs, check_vma=False
    )
```

time: 119 us -> 75.4 us (0.63)
  the two profiles are of different devices: /device:TPU:24 before, /device:TPU:1 now
where the time goes in v1:
time: 75.4 us; the launch traced here: 75 us
  starting transfers between devices  52.5 us (70%)
  Pallas kernels  13.1 us (17%)
  waiting for transfers between devices  5.42 us (7%)
  local copies, waits for them, and re-layouts  3.28 us (4%)
    ppermute x4, starting transfers between devices, exchange(): return lax.ppermute(value, axis, pairs)  37.8 us
    ppermute x1, starting transfers between devices, per_device(): after = lax.ppermute(panels, both, down)  11.6 us
    pallas_call x4, Pallas kernels, combine(): pl.pallas_call(functools.partial(level_body, level, ordered), grid=(1,),...  9.38 us
    ppermute x4, waiting for transfers between devices, exchange(): return lax.ppermute(value, axis, pairs)  5.41 us
    pallas_call x1, Pallas kernels, near_sums(): pl.pallas_call(near_body, out_shape=jax.ShapeDtypeStruct(own.shape, own.d...  3.72 us
    unnamed x14, local copies, waits for them, and re-layouts  3.28 us
    ppermute x1, starting transfers between devices, per_device(): before = lax.ppermute(panels, both, up)  3.12 us
  transfers between devices with their start and end apart: 6, of which 2 were waited for; matrix products, arithmetic and copies ran while one was open for 0% of the time, Pallas kernels for 8%

profile of v1, /device:TPU:1, one launch (start us, length us, event | category | flops | bytes accessed | tf_op | source)
XLA Modules:
  0.0 75.0 jit_solution(10192101427370676473)
XLA Ops:
  0.6 0.0 copy-start
  0.6 16.4 %collective-permute-start = (bf16[32,2048]{1,0:T(8,128)(2,1)}, bf16[32,2048]{1,0:T(8,128)(2,1)S(1)}, u32[]{:S(2)}, u32[]{:S(2)}) collective-permute-start(bf16[32,2048]{1,0:T(8,128)(2,1)} %own.2), channel_id=1, source_target_pairs={{0,16},{1,17},{2,18},{3,19},{4,20},{5,21},{6,22},{7,23},{8,24},{9,... | collective-permute-start | bytes 393224 | tf_op jit(solution)/shard_map/ppermute | solution.py:16
  17.1 2.9 %collective-permute-done.partner = bf16[32,2048]{1,0:T(8,128)(2,1)S(1)} collective-permute-done((bf16[32,2048]{1,0:T(8,128)(2,1)}, bf16[32,2048]{1,0:T(8,128)(2,1)S(1)}, u32[]{:S(2)}, u32[]{:S(2)}) %collective-permute-start) | collective-permute-done | bytes 131104 | tf_op jit(solution)/shard_map/ppermute | solution.py:16
  19.9 0.0 copy-start.6
  19.9 0.7 copy-done.6
  20.6 2.3 %level0.1.own = bf16[32,2048]{1,0:T(8,128)(2,1)} custom-call(s32[4,32]{1,0:T(4,128)} %pattern.7, s32[32]{0:T(128)} %order.7, bf16[32,2048]{1,0:T(8,128)(2,1)} %own.2, bf16[32,2048]{1,0:T(8,128)(2,1)} %copy-done.6, bf16[4,32,64,128]{3,2,1,0:T(8,128)(2,1)} %bitcast.3), custom_call_target="tpu_custom_call" | custom-call | flops 16777216 | bytes 1048576 | tf_op jit(solution)/shard_map/level0/pallas_call | solution.py:63
  22.9 5.2 %collective-permute-start.1 = (bf16[32,2048]{1,0:T(8,128)(2,1)}, bf16[32,2048]{1,0:T(8,128)(2,1)S(1)}, u32[]{:S(2)}, u32[]{:S(2)}) collective-permute-start(bf16[32,2048]{1,0:T(8,128)(2,1)} %level0.1.own), channel_id=1, source_target_pairs={{0,256},{32,288},{64,320},{96,352},{128,384},{160,416},{192,448},{... | collective-permute-start | bytes 393224 | tf_op jit(solution)/shard_map/ppermute | solution.py:16
  28.1 2.6 %collective-permute-done.1.partner = bf16[32,2048]{1,0:T(8,128)(2,1)S(1)} collective-permute-done((bf16[32,2048]{1,0:T(8,128)(2,1)}, bf16[32,2048]{1,0:T(8,128)(2,1)S(1)}, u32[]{:S(2)}, u32[]{:S(2)}) %collective-permute-start.1) | collective-permute-done | bytes 131104 | tf_op jit(solution)/shard_map/ppermute | solution.py:16
  30.7 0.0 copy-start.5
  30.7 0.7 copy-done.5
  31.3 2.3 %level1.1.own = bf16[32,2048]{1,0:T(8,128)(2,1)} custom-call(s32[4,32]{1,0:T(4,128)} %pattern.7, s32[32]{0:T(128)} %order.7, bf16[32,2048]{1,0:T(8,128)(2,1)} %level0.1.own, bf16[32,2048]{1,0:T(8,128)(2,1)} %copy-done.5, bf16[4,32,64,128]{3,2,1,0:T(8,128)(2,1)} %bitcast.4), custom_call_target="tpu_custom_call" | custom-call | flops 16777216 | bytes 1048576 | tf_op jit(solution)/shard_map/level1/pallas_call | solution.py:63
  33.7 11.3 %collective-permute-start.2 = (bf16[32,2048]{1,0:T(8,128)(2,1)}, bf16[32,2048]{1,0:T(8,128)(2,1)S(1)}, u32[]{:S(2)}, u32[]{:S(2)}) collective-permute-start(bf16[32,2048]{1,0:T(8,128)(2,1)} %level1.1.own), channel_id=1, source_target_pairs={{0,8},{1,9},{2,10},{3,11},{4,12},{5,13},{6,14},{7,15},{8,0},{9,1},... | collective-permute-start | bytes 393224 | tf_op jit(solution)/shard_map/ppermute | solution.py:16
  45.0 0.0 copy-done
  45.0 3.1 %collective-permute-start.4 = (bf16[32,2048]{1,0:T(8,128)(2,1)S(1)}, bf16[32,2048]{1,0:T(8,128)(2,1)S(1)}, u32[]{:S(2)}, u32[]{:S(2)}) collective-permute-start(bf16[32,2048]{1,0:T(8,128)(2,1)S(1)} %copy-done), channel_id=1, source_target_pairs={{0,1},{1,2},{2,3},{3,4},{4,5},{5,6},{6,7},{7,8},{8,9},{9,10},{10,1... | collective-permute-start | bytes 393224 | tf_op jit(solution)/shard_map/ppermute | solution.py:150
  48.2 11.6 %collective-permute-start.5 = (bf16[32,2048]{1,0:T(8,128)(2,1)S(1)}, bf16[32,2048]{1,0:T(8,128)(2,1)S(1)}, u32[]{:S(2)}, u32[]{:S(2)}) collective-permute-start(bf16[32,2048]{1,0:T(8,128)(2,1)S(1)} %copy-done), channel_id=1, source_target_pairs={{1,0},{2,1},{3,2},{4,3},{5,4},{6,5},{7,6},{8,7},{9,8},{10,9},{11,1... | collective-permute-start | bytes 393224 | tf_op jit(solution)/shard_map/ppermute | solution.py:151
  59.8 0.0 collective-permute-done.2.partner
  59.8 0.0 copy-start.4
  59.8 0.6 copy-done.4
  60.4 2.3 %level2.1.own = bf16[32,2048]{1,0:T(8,128)(2,1)} custom-call(s32[4,32]{1,0:T(4,128)} %pattern.7, s32[32]{0:T(128)} %order.7, bf16[32,2048]{1,0:T(8,128)(2,1)} %level1.1.own, bf16[32,2048]{1,0:T(8,128)(2,1)} %copy-done.4, bf16[4,32,64,128]{3,2,1,0:T(8,128)(2,1)} %bitcast.5), custom_call_target="tpu_custom_call" | custom-call | flops 16777216 | bytes 1048576 | tf_op jit(solution)/shard_map/level2/pallas_call | solution.py:63
  62.8 4.8 %collective-permute-start.3 = (bf16[32,2048]{1,0:T(8,128)(2,1)}, bf16[32,2048]{1,0:T(8,128)(2,1)S(1)}, u32[]{:S(2)}, u32[]{:S(2)}) collective-permute-start(bf16[32,2048]{1,0:T(8,128)(2,1)} %level2.1.own), channel_id=1, source_target_pairs={{0,128},{32,160},{64,192},{96,224},{128,0},{160,32},{192,64},{224,... | collective-permute-start | bytes 393224 | tf_op jit(solution)/shard_map/ppermute | solution.py:16
  67.6 0.0 collective-permute-done.4.before
  67.6 0.0 copy-start.1
  67.6 0.0 collective-permute-done.5.after
  67.6 0.0 copy-start.2
  67.6 0.6 copy-done.1
  68.3 0.0 copy-done.2
  68.3 3.7 %near.1 = bf16[32,2048]{1,0:T(8,128)(2,1)} custom-call(s32[1]{0:T(128)} %bitcast.1.first, s32[6,32]{1,0:T(8,128)} %bitcast.7, bf16[32,2048]{1,0:T(8,128)(2,1)} %copy-done.1, bf16[32,2048]{1,0:T(8,128)(2,1)} %own.3, bf16[32,2048]{1,0:T(8,128)(2,1)} %copy-done.2, bf16[32,6,64,64]{3,2,1,0:T(8,128)(2,1)} %matrices.1), custom_call_target="tpu_custom_call" | custom-call | flops 50331648 | bytes 4194304 | tf_op jit(solution)/shard_map/near/pallas_call | solution.py:118
  72.0 0.0 collective-permute-done.3.partner
  72.0 0.0 copy-start.3
  72.0 0.6 copy-done.3
  72.7 2.3 %level3.1 = bf16[32,2048]{1,0:T(8,128)(2,1)} custom-call(s32[4,32]{1,0:T(4,128)} %pattern.7, s32[32]{0:T(128)} %order.7, bf16[32,2048]{1,0:T(8,128)(2,1)} %level2.1.own, bf16[32,2048]{1,0:T(8,128)(2,1)} %copy-done.3, bf16[4,32,64,128]{3,2,1,0:T(8,128)(2,1)} %bitcast.6), custom_call_target="tpu_custom_call" | custom-call | flops 16777216 | bytes 1048576 | tf_op jit(solution)/shard_map/level3/pallas_call | solution.py:63
Async XLA Ops:
  0.6 44.4 %copy-start = (bf16[32,2048]{1,0:T(8,128)(2,1)S(1)}, bf16[32,2048]{1,0:T(8,128)(2,1)}, u32[]{:S(2)}) copy-start(bf16[32,2048]{1,0:T(8,128)(2,1)} %own.3) | copy-start | bytes 393220
  0.6 19.3 %collective-permute-start = (bf16[32,2048]{1,0:T(8,128)(2,1)}, bf16[32,2048]{1,0:T(8,128)(2,1)S(1)}, u32[]{:S(2)}, u32[]{:S(2)}) collective-permute-start(bf16[32,2048]{1,0:T(8,128)(2,1)} %own.2), channel_id=1, source_target_pairs={{0,16},{1,17},{2,18},{3,19},{4,20},{5,21},{6,22},{7,23},{8,24},{9,... | collective-permute-start | bytes 393224 | tf_op jit(solution)/shard_map/ppermute | solution.py:16
  19.9 0.7 copy-start.6
  22.9 7.8 %collective-permute-start.1 = (bf16[32,2048]{1,0:T(8,128)(2,1)}, bf16[32,2048]{1,0:T(8,128)(2,1)S(1)}, u32[]{:S(2)}, u32[]{:S(2)}) collective-permute-start(bf16[32,2048]{1,0:T(8,128)(2,1)} %level0.1.own), channel_id=1, source_target_pairs={{0,256},{32,288},{64,320},{96,352},{128,384},{160,416},{192,448},{... | collective-permute-start | bytes 393224 | tf_op jit(solution)/shard_map/ppermute | solution.py:16
  30.7 0.7 copy-start.5
  33.7 26.1 %collective-permute-start.2 = (bf16[32,2048]{1,0:T(8,128)(2,1)}, bf16[32,2048]{1,0:T(8,128)(2,1)S(1)}, u32[]{:S(2)}, u32[]{:S(2)}) collective-permute-start(bf16[32,2048]{1,0:T(8,128)(2,1)} %level1.1.own), channel_id=1, source_target_pairs={{0,8},{1,9},{2,10},{3,11},{4,12},{5,13},{6,14},{7,15},{8,0},{9,1},... | collective-permute-start | bytes 393224 | tf_op jit(solution)/shard_map/ppermute | solution.py:16
  45.0 22.6 %collective-permute-start.4 = (bf16[32,2048]{1,0:T(8,128)(2,1)S(1)}, bf16[32,2048]{1,0:T(8,128)(2,1)S(1)}, u32[]{:S(2)}, u32[]{:S(2)}) collective-permute-start(bf16[32,2048]{1,0:T(8,128)(2,1)S(1)} %copy-done), channel_id=1, source_target_pairs={{0,1},{1,2},{2,3},{3,4},{4,5},{5,6},{6,7},{7,8},{8,9},{9,10},{10,1... | collective-permute-start | bytes 393224 | tf_op jit(solution)/shard_map/ppermute | solution.py:150
  48.2 19.5 %collective-permute-start.5 = (bf16[32,2048]{1,0:T(8,128)(2,1)S(1)}, bf16[32,2048]{1,0:T(8,128)(2,1)S(1)}, u32[]{:S(2)}, u32[]{:S(2)}) collective-permute-start(bf16[32,2048]{1,0:T(8,128)(2,1)S(1)} %copy-done), channel_id=1, source_target_pairs={{1,0},{2,1},{3,2},{4,3},{5,4},{6,5},{7,6},{8,7},{9,8},{10,9},{11,1... | collective-permute-start | bytes 393224 | tf_op jit(solution)/shard_map/ppermute | solution.py:151
  59.8 0.7 copy-start.4
  62.8 9.2 %collective-permute-start.3 = (bf16[32,2048]{1,0:T(8,128)(2,1)}, bf16[32,2048]{1,0:T(8,128)(2,1)S(1)}, u32[]{:S(2)}, u32[]{:S(2)}) collective-permute-start(bf16[32,2048]{1,0:T(8,128)(2,1)} %level2.1.own), channel_id=1, source_target_pairs={{0,128},{32,160},{64,192},{96,224},{128,0},{160,32},{192,64},{224,... | collective-permute-start | bytes 393224 | tf_op jit(solution)/shard_map/ppermute | solution.py:16
  67.6 0.7 copy-start.1
  67.6 0.7 copy-start.2
  72.0 0.6 copy-start.3

commit v2 on v1

--- a/solution.py
+++ b/solution.py
@@ -8,6 +8,7 @@
 from jax.sharding import PartitionSpec as P
 
 LANES = 128
+MIB = 1 << 20
 NT = (((1,), (1,)), ((), ()))
 
 
@@ -75,8 +76,38 @@
         cost_estimate=pl.CostEstimate(
             flops=2 * own.size * depth, bytes_accessed=1 << 20, transcendentals=0
         ),
+        compiler_params=pltpu.CompilerParams(vmem_limit_bytes=4 * MIB),
         name=f"level{level}",
     )(pattern, order, own, partner, matrices)
+
+
+def stage_body(*refs):
+    count = (len(refs) - 1) // 2
+    sources, targets, sems = refs[:count], refs[count : 2 * count], refs[-1]
+    copies = [
+        pltpu.make_async_copy(source, target, sems.at[i])
+        for i, (source, target) in enumerate(zip(sources, targets))
+    ]
+    for copy in copies:
+        copy.start()
+    for copy in copies:
+        copy.wait()
+
+
+def staged(*arrays):
+    hbm = pl.BlockSpec(memory_space=pltpu.HBM)
+    vmem = pl.BlockSpec(memory_space=pltpu.VMEM)
+    size = sum(a.size * a.dtype.itemsize for a in arrays)
+    return pl.pallas_call(
+        stage_body,
+        out_shape=[jax.ShapeDtypeStruct(a.shape, a.dtype) for a in arrays],
+        in_specs=[hbm] * len(arrays),
+        out_specs=[vmem] * len(arrays),
+        scratch_shapes=[pltpu.SemaphoreType.DMA((len(arrays),))],
+        cost_estimate=pl.CostEstimate(flops=0, bytes_accessed=2 * size, transcendentals=0),
+        compiler_params=pltpu.CompilerParams(vmem_limit_bytes=8 * MIB),
+        name="stage",
+    )(*(pltpu.with_memory_space_constraint(a, pltpu.HBM) for a in arrays))
 
 
 def near_body(first, neighbors, before, own, after, matrices, out, held):
@@ -124,6 +155,7 @@
         cost_estimate=pl.CostEstimate(
             flops=2 * own.size * 384, bytes_accessed=4 << 20, transcendentals=0
         ),
+        compiler_params=pltpu.CompilerParams(vmem_limit_bytes=8 * MIB),
         name="near",
     )(first, neighbors, before, own, after, matrices)
 
@@ -132,23 +164,28 @@
     boxes = pattern.shape[1]
     col_bits = lax.axis_size("col").bit_length() - 1
     row_bits = lax.axis_size("row").bit_length() - 1
+    both = ("row", "col")
+    count = lax.axis_size(both)
+    up = [(i, i + 1) for i in range(count - 1)]
+    down = [(j, i) for i, j in up]
+    partner = exchange(coefficients, "col", 1 << (col_bits - 1))
+    before = lax.ppermute(panels, both, up)
+    after = lax.ppermute(panels, both, down)
     matrices = jnp.swapaxes(factors, 2, 3)
-    blocks = coefficients
+    blocks, matrices, pattern, octree_order = staged(
+        coefficients, matrices, pattern, octree_order
+    )
     levels = factors.shape[0]
     for level in range(levels):
-        if level % 2 == 0:
+        if level == 0:
+            pass
+        elif level % 2 == 0:
             partner = exchange(blocks, "col", 1 << (col_bits - 1 - level // 2))
         else:
             partner = exchange(blocks, "row", 1 << (row_bits - 1 - level // 2))
         blocks = combine(
             level, level == levels - 1, pattern, octree_order, blocks, partner, matrices
         )
-    both = ("row", "col")
-    count = lax.axis_size(both)
-    up = [(i, i + 1) for i in range(count - 1)]
-    down = [(j, i) for i, j in up]
-    before = lax.ppermute(panels, both, up)
-    after = lax.ppermute(panels, both, down)
     first = (lax.axis_index(both) * boxes - boxes).astype(jnp.int32).reshape(1)
     near_field = near_sums(
         first, jnp.swapaxes(neighbors, 0, 1), before, panels, after, near_blocks

time: 75.4 us -> 67.7 us (0.90)
  Pallas kernels: 13.1 us -> 8.86 us
  waiting for transfers between devices: 5.42 us -> 3.49 us
  local copies, waits for them, and re-layouts: 3.28 us -> 1.89 us
    pallas_call x4, Pallas kernels: 9.38 us -> 4.94 us  [combine(): pl.pallas_call(functools.partial(level_body, level, ordered), grid=(1,),...]
    ppermute x4, waiting for transfers between devices: 5.41 us -> 3.48 us  [exchange(): return lax.ppermute(value, axis, pairs)]
    pallas_call x0 -> x1, Pallas kernels: none -> 1.71 us  [staged(): pl.pallas_call(stage_body, out_shape=[jax.ShapeDtypeStruct(a.shape, a.dty...]
    pallas_call x1, Pallas kernels: 3.72 us -> 2.21 us  [near_sums(): pl.pallas_call(near_body, out_shape=jax.ShapeDtypeStruct(own.shape, own.d...]
    unnamed x14 -> x6, local copies, waits for them, and re-layouts: 3.28 us -> 1.89 us
  transfers between devices with their start and end apart: 6 -> 6, of which waited for: 2 -> 2; matrix products, arithmetic and copies ran while one was open for 0% -> 0% of each run, Pallas kernels for 8% -> 7%
where the time goes in v2:
time: 67.7 us; the launch traced here: 67.4 us
  starting transfers between devices  52.4 us (77%)
  Pallas kernels  8.86 us (13%)
  waiting for transfers between devices  3.49 us (5%)
  local copies, waits for them, and re-layouts  1.89 us (3%)
  between operations  0.77 us (1%)
    ppermute x4, starting transfers between devices, exchange(): return lax.ppermute(value, axis, pairs)  37.7 us
    ppermute x1, starting transfers between devices, per_device(): after = lax.ppermute(panels, both, down)  11.6 us
    pallas_call x4, Pallas kernels, combine(): pl.pallas_call(functools.partial(level_body, level, ordered), grid=(1,),...  4.94 us
    ppermute x4, waiting for transfers between devices, exchange(): return lax.ppermute(value, axis, pairs)  3.48 us
    ppermute x1, starting transfers between devices, per_device(): before = lax.ppermute(panels, both, up)  3.12 us
    pallas_call x1, Pallas kernels, near_sums(): pl.pallas_call(near_body, out_shape=jax.ShapeDtypeStruct(own.shape, own.d...  2.21 us
    unnamed x6, local copies, waits for them, and re-layouts  1.89 us
    pallas_call x1, Pallas kernels, staged(): pl.pallas_call(stage_body, out_shape=[jax.ShapeDtypeStruct(a.shape, a.dty...  1.71 us
  transfers between devices with their start and end apart: 6, of which 2 were waited for; matrix products, arithmetic and copies ran while one was open for 0% of the time, Pallas kernels for 7%

profile of v2, /device:TPU:1, one launch (start us, length us, event | category | flops | bytes accessed | tf_op | source)
XLA Modules:
  0.0 67.4 jit_solution(13426780734832449108)
XLA Ops:
  0.6 16.3 %collective-permute-start = (bf16[32,2048]{1,0:T(8,128)(2,1)}, bf16[32,2048]{1,0:T(8,128)(2,1)S(1)}, u32[]{:S(2)}, u32[]{:S(2)}) collective-permute-start(bf16[32,2048]{1,0:T(8,128)(2,1)} %refs_0_.1), channel_id=1, source_target_pairs={{0,16},{1,17},{2,18},{3,19},{4,20},{5,21},{6,22},{7,23},{8,24},{9,... | collective-permute-start | bytes 393224 | tf_op jit(solution)/shard_map/ppermute | solution.py:17
  16.9 1.7 %stage.1 = (bf16[32,2048]{1,0:T(8,128)(2,1)S(1)}, bf16[4,32,64,128]{3,2,1,0:T(8,128)(2,1)S(1)}, s32[4,32]{1,0:T(4,128)S(1)}, s32[32]{0:T(128)S(1)}) custom-call(bf16[32,2048]{1,0:T(8,128)(2,1)} %refs_0_.1, bf16[4,32,64,128]{3,2,1,0:T(8,128)(2,1)} %bitcast.4, s32[4,32]{1,0:T(4,128)} %refs_2_.1, s32[32]{0:T(128)} %refs_3_.1), custom_call_target="tpu_custom_call" | custom-call | bytes 4457728 | tf_op jit(solution)/shard_map/stage/pallas_call | solution.py:101
  18.6 1.1 %collective-permute-done.partner = bf16[32,2048]{1,0:T(8,128)(2,1)S(1)} collective-permute-done((bf16[32,2048]{1,0:T(8,128)(2,1)}, bf16[32,2048]{1,0:T(8,128)(2,1)S(1)}, u32[]{:S(2)}, u32[]{:S(2)}) %collective-permute-start) | collective-permute-done | bytes 131104 | tf_op jit(solution)/shard_map/ppermute | solution.py:17
  19.8 0.0 copy-start.1
  19.8 1.1 %level0.1.own = bf16[32,2048]{1,0:T(8,128)(2,1)S(1)} custom-call(s32[4,32]{1,0:T(4,128)S(1)} %get-tuple-element.6.pattern, s32[32]{0:T(128)S(1)} %get-tuple-element.7.order, bf16[32,2048]{1,0:T(8,128)(2,1)S(1)} %get-tuple-element.8.own, bf16[32,2048]{1,0:T(8,128)(2,1)S(1)} %collective-permute-done.partner, bf16[4,32,64,128]{3,2,1,0:T(8,128)(2,1)S(1)} %get-tuple-element.9.matrices), custom_call_target="tpu_custom_call" | custom-call | flops 16777216 | bytes 1048576 | tf_op jit(solution)/shard_map/level0/pallas_call | solution.py:64
  20.8 0.0 copy-start.2
  20.9 5.2 %collective-permute-start.1 = (bf16[32,2048]{1,0:T(8,128)(2,1)S(1)}, bf16[32,2048]{1,0:T(8,128)(2,1)S(1)}, u32[]{:S(2)}, u32[]{:S(2)}) collective-permute-start(bf16[32,2048]{1,0:T(8,128)(2,1)S(1)} %level0.1.own), channel_id=1, source_target_pairs={{0,256},{32,288},{64,320},{96,352},{128,384},{160,416},{192,448},{... | collective-permute-start | bytes 393224 | tf_op jit(solution)/shard_map/ppermute | solution.py:17
  26.1 2.3 %collective-permute-done.1.partner = bf16[32,2048]{1,0:T(8,128)(2,1)S(1)} collective-permute-done((bf16[32,2048]{1,0:T(8,128)(2,1)S(1)}, bf16[32,2048]{1,0:T(8,128)(2,1)S(1)}, u32[]{:S(2)}, u32[]{:S(2)}) %collective-permute-start.1) | collective-permute-done | bytes 131104 | tf_op jit(solution)/shard_map/ppermute | solution.py:17
  28.4 1.1 %level1.1.own = bf16[32,2048]{1,0:T(8,128)(2,1)S(1)} custom-call(s32[4,32]{1,0:T(4,128)S(1)} %get-tuple-element.6.pattern, s32[32]{0:T(128)S(1)} %get-tuple-element.7.order, bf16[32,2048]{1,0:T(8,128)(2,1)S(1)} %level0.1.own, bf16[32,2048]{1,0:T(8,128)(2,1)S(1)} %collective-permute-done.1.partner, bf16[4,32,64,128]{3,2,1,0:T(8,128)(2,1)S(1)} %get-tuple-element.9.matrices), custom_call_target="tpu_custom_call" | custom-call | flops 16777216 | bytes 1048576 | tf_op jit(solution)/shard_map/level1/pallas_call | solution.py:64
  29.5 11.3 %collective-permute-start.2 = (bf16[32,2048]{1,0:T(8,128)(2,1)S(1)}, bf16[32,2048]{1,0:T(8,128)(2,1)S(1)}, u32[]{:S(2)}, u32[]{:S(2)}) collective-permute-start(bf16[32,2048]{1,0:T(8,128)(2,1)S(1)} %level1.1.own), channel_id=1, source_target_pairs={{0,8},{1,9},{2,10},{3,11},{4,12},{5,13},{6,14},{7,15},{8,0},{9,1},... | collective-permute-start | bytes 393224 | tf_op jit(solution)/shard_map/ppermute | solution.py:17
  40.9 0.0 copy-done.1
  40.9 3.1 %collective-permute-start.4 = (bf16[32,2048]{1,0:T(8,128)(2,1)S(1)}, bf16[32,2048]{1,0:T(8,128)(2,1)S(1)}, u32[]{:S(2)}, u32[]{:S(2)}) collective-permute-start(bf16[32,2048]{1,0:T(8,128)(2,1)S(1)} %copy-done.1), channel_id=1, source_target_pairs={{0,1},{1,2},{2,3},{3,4},{4,5},{5,6},{6,7},{7,8},{8,9},{9,10},{10,1... | collective-permute-start | bytes 393224 | tf_op jit(solution)/shard_map/ppermute | solution.py:172
  44.0 11.6 %collective-permute-start.5 = (bf16[32,2048]{1,0:T(8,128)(2,1)S(1)}, bf16[32,2048]{1,0:T(8,128)(2,1)S(1)}, u32[]{:S(2)}, u32[]{:S(2)}) collective-permute-start(bf16[32,2048]{1,0:T(8,128)(2,1)S(1)} %copy-done.1), channel_id=1, source_target_pairs={{1,0},{2,1},{3,2},{4,3},{5,4},{6,5},{7,6},{8,7},{9,8},{10,9},{11,1... | collective-permute-start | bytes 393224 | tf_op jit(solution)/shard_map/ppermute | solution.py:173
  55.6 0.0 collective-permute-done.2.partner
  55.6 1.1 %level2.1.own = bf16[32,2048]{1,0:T(8,128)(2,1)S(1)} custom-call(s32[4,32]{1,0:T(4,128)S(1)} %get-tuple-element.6.pattern, s32[32]{0:T(128)S(1)} %get-tuple-element.7.order, bf16[32,2048]{1,0:T(8,128)(2,1)S(1)} %level1.1.own, bf16[32,2048]{1,0:T(8,128)(2,1)S(1)} %collective-permute-done.2.partner, bf16[4,32,64,128]{3,2,1,0:T(8,128)(2,1)S(1)} %get-tuple-element.9.matrices), custom_call_target="tpu_custom_call" | custom-call | flops 16777216 | bytes 1048576 | tf_op jit(solution)/shard_map/level2/pallas_call | solution.py:64
  56.7 4.8 %collective-permute-start.3 = (bf16[32,2048]{1,0:T(8,128)(2,1)S(1)}, bf16[32,2048]{1,0:T(8,128)(2,1)S(1)}, u32[]{:S(2)}, u32[]{:S(2)}) collective-permute-start(bf16[32,2048]{1,0:T(8,128)(2,1)S(1)} %level2.1.own), channel_id=1, source_target_pairs={{0,128},{32,160},{64,192},{96,224},{128,0},{160,32},{192,64},{224,... | collective-permute-start | bytes 393224 | tf_op jit(solution)/shard_map/ppermute | solution.py:17
  61.5 0.0 collective-permute-done.4.before
  61.5 0.0 collective-permute-done.5.after
  61.5 0.0 copy-done.2
  61.5 0.0 copy-start
  61.6 1.9 %copy-done = bf16[32,6,64,64]{3,2,1,0:T(8,128)(2,1)S(1)} copy-done((bf16[32,6,64,64]{3,2,1,0:T(8,128)(2,1)S(1)}, bf16[32,6,64,64]{3,2,1,0:T(8,128)(2,1)}, u32[]{:S(2)}) %copy-start) | copy-done | bytes 1572888
  63.4 2.2 %near.1 = bf16[32,2048]{1,0:T(8,128)(2,1)} custom-call(s32[1]{0:T(128)} %bitcast.1.first, s32[6,32]{1,0:T(8,128)S(1)} %bitcast.3, bf16[32,2048]{1,0:T(8,128)(2,1)S(1)} %collective-permute-done.4.before, bf16[32,2048]{1,0:T(8,128)(2,1)S(1)} %copy-done.1, bf16[32,2048]{1,0:T(8,128)(2,1)S(1)} %collective-permute-done.5.after, bf16[32,6,64,64]{3,2,1,0:T(8,128)(2,1)S(1)} %copy-done), custom_call_target="tpu_custom_call" | custom-call | flops 50331648 | bytes 4194304 | tf_op jit(solution)/shard_map/near/pallas_call | solution.py:149
  65.6 0.0 collective-permute-done.3.partner
  65.6 1.7 %level3.1 = bf16[32,2048]{1,0:T(8,128)(2,1)} custom-call(s32[4,32]{1,0:T(4,128)S(1)} %get-tuple-element.6.pattern, s32[32]{0:T(128)S(1)} %get-tuple-element.7.order, bf16[32,2048]{1,0:T(8,128)(2,1)S(1)} %level2.1.own, bf16[32,2048]{1,0:T(8,128)(2,1)S(1)} %collective-permute-done.3.partner, bf16[4,32,64,128]{3,2,1,0:T(8,128)(2,1)S(1)} %get-tuple-element.9.matrices), custom_call_target="tpu_custom_call" | custom-call | flops 16777216 | bytes 1048576 | tf_op jit(solution)/shard_map/level3/pallas_call | solution.py:64
Async XLA Ops:
  0.6 19.1 %collective-permute-start = (bf16[32,2048]{1,0:T(8,128)(2,1)}, bf16[32,2048]{1,0:T(8,128)(2,1)S(1)}, u32[]{:S(2)}, u32[]{:S(2)}) collective-permute-start(bf16[32,2048]{1,0:T(8,128)(2,1)} %refs_0_.1), channel_id=1, source_target_pairs={{0,16},{1,17},{2,18},{3,19},{4,20},{5,21},{6,22},{7,23},{8,24},{9,... | collective-permute-start | bytes 393224 | tf_op jit(solution)/shard_map/ppermute | solution.py:17
  19.8 21.1 %copy-start.1 = (bf16[32,2048]{1,0:T(8,128)(2,1)S(1)}, bf16[32,2048]{1,0:T(8,128)(2,1)}, u32[]{:S(2)}) copy-start(bf16[32,2048]{1,0:T(8,128)(2,1)} %own.1) | copy-start | bytes 393220
  20.8 40.7 %copy-start.2 = (s32[32,6]{0,1:T(8,128)S(1)}, s32[32,6]{0,1:T(8,128)}, u32[]{:S(2)}) copy-start(s32[32,6]{0,1:T(8,128)} %param.13) | copy-start | bytes 2308
  20.9 7.6 %collective-permute-start.1 = (bf16[32,2048]{1,0:T(8,128)(2,1)S(1)}, bf16[32,2048]{1,0:T(8,128)(2,1)S(1)}, u32[]{:S(2)}, u32[]{:S(2)}) collective-permute-start(bf16[32,2048]{1,0:T(8,128)(2,1)S(1)} %level0.1.own), channel_id=1, source_target_pairs={{0,256},{32,288},{64,320},{96,352},{128,384},{160,416},{192,448},{... | collective-permute-start | bytes 393224 | tf_op jit(solution)/shard_map/ppermute | solution.py:17
  29.5 26.1 %collective-permute-start.2 = (bf16[32,2048]{1,0:T(8,128)(2,1)S(1)}, bf16[32,2048]{1,0:T(8,128)(2,1)S(1)}, u32[]{:S(2)}, u32[]{:S(2)}) collective-permute-start(bf16[32,2048]{1,0:T(8,128)(2,1)S(1)} %level1.1.own), channel_id=1, source_target_pairs={{0,8},{1,9},{2,10},{3,11},{4,12},{5,13},{6,14},{7,15},{8,0},{9,1},... | collective-permute-start | bytes 393224 | tf_op jit(solution)/shard_map/ppermute | solution.py:17
  40.9 20.7 %collective-permute-start.4 = (bf16[32,2048]{1,0:T(8,128)(2,1)S(1)}, bf16[32,2048]{1,0:T(8,128)(2,1)S(1)}, u32[]{:S(2)}, u32[]{:S(2)}) collective-permute-start(bf16[32,2048]{1,0:T(8,128)(2,1)S(1)} %copy-done.1), channel_id=1, source_target_pairs={{0,1},{1,2},{2,3},{3,4},{4,5},{5,6},{6,7},{7,8},{8,9},{9,10},{10,1... | collective-permute-start | bytes 393224 | tf_op jit(solution)/shard_map/ppermute | solution.py:172
  44.0 17.5 %collective-permute-start.5 = (bf16[32,2048]{1,0:T(8,128)(2,1)S(1)}, bf16[32,2048]{1,0:T(8,128)(2,1)S(1)}, u32[]{:S(2)}, u32[]{:S(2)}) collective-permute-start(bf16[32,2048]{1,0:T(8,128)(2,1)S(1)} %copy-done.1), channel_id=1, source_target_pairs={{1,0},{2,1},{3,2},{4,3},{5,4},{6,5},{7,6},{8,7},{9,8},{10,9},{11,1... | collective-permute-start | bytes 393224 | tf_op jit(solution)/shard_map/ppermute | solution.py:173
  56.7 9.0 %collective-permute-start.3 = (bf16[32,2048]{1,0:T(8,128)(2,1)S(1)}, bf16[32,2048]{1,0:T(8,128)(2,1)S(1)}, u32[]{:S(2)}, u32[]{:S(2)}) collective-permute-start(bf16[32,2048]{1,0:T(8,128)(2,1)S(1)} %level2.1.own), channel_id=1, source_target_pairs={{0,128},{32,160},{64,192},{96,224},{128,0},{160,32},{192,64},{224,... | collective-permute-start | bytes 393224 | tf_op jit(solution)/shard_map/ppermute | solution.py:17
  61.5 1.9 %copy-start = (bf16[32,6,64,64]{3,2,1,0:T(8,128)(2,1)S(1)}, bf16[32,6,64,64]{3,2,1,0:T(8,128)(2,1)}, u32[]{:S(2)}) copy-start(bf16[32,6,64,64]{3,2,1,0:T(8,128)(2,1)} %matrices.1) | copy-start | bytes 4718596

commit v3 on v2

--- a/solution.py
+++ b/solution.py
@@ -30,7 +30,7 @@
 
 def level_body(level, ordered, pattern, order, own, partner, matrices, out):
     rows = own.shape[0]
-    boxes = matrices.shape[0]
+    boxes = matrices.shape[1]
     low = lax.broadcasted_iota(jnp.int32, (rows, LANES), 1) < LANES // 2
     for pair in range(boxes // 2):
         sides = []
@@ -46,7 +46,7 @@
             q = pattern[level, box]
             theirs = placed(tile_of(partner, q), q, True)
             sides.append(jnp.where(low, mine, theirs))
-            weights.append(matrices[box])
+            weights.append(matrices[level, box])
         product = lax.dot_general(
             jnp.concatenate(sides, axis=0),
             jnp.concatenate(weights, axis=0),
@@ -58,20 +58,13 @@
 
 
 def combine(level, ordered, pattern, order, own, partner, matrices):
-    _, boxes, rank, depth = matrices.shape
+    depth = matrices.shape[3]
     smem = pl.BlockSpec(memory_space=pltpu.SMEM)
     vmem = pl.BlockSpec(memory_space=pltpu.VMEM)
     return pl.pallas_call(
         functools.partial(level_body, level, ordered),
-        grid=(1,),
         out_shape=jax.ShapeDtypeStruct(own.shape, own.dtype),
-        in_specs=[
-            smem,
-            smem,
-            vmem,
-            vmem,
-            pl.BlockSpec((None, boxes, rank, depth), lambda i: (level, 0, 0, 0)),
-        ],
+        in_specs=[smem, smem, vmem, vmem, vmem],
         out_specs=vmem,
         cost_estimate=pl.CostEstimate(
             flops=2 * own.size * depth, bytes_accessed=1 << 20, transcendentals=0
@@ -94,42 +87,55 @@
         copy.wait()
 
 
-def staged(*arrays):
+def staged(indices, arrays):
     hbm = pl.BlockSpec(memory_space=pltpu.HBM)
+    smem = pl.BlockSpec(memory_space=pltpu.SMEM)
     vmem = pl.BlockSpec(memory_space=pltpu.VMEM)
     size = sum(a.size * a.dtype.itemsize for a in arrays)
+    total = len(indices) + len(arrays)
     return pl.pallas_call(
         stage_body,
-        out_shape=[jax.ShapeDtypeStruct(a.shape, a.dtype) for a in arrays],
-        in_specs=[hbm] * len(arrays),
-        out_specs=[vmem] * len(arrays),
-        scratch_shapes=[pltpu.SemaphoreType.DMA((len(arrays),))],
+        out_shape=[pltpu.SMEM(a.shape, a.dtype) for a in indices]
+        + [jax.ShapeDtypeStruct(a.shape, a.dtype) for a in arrays],
+        in_specs=[hbm] * total,
+        out_specs=[smem] * len(indices) + [vmem] * len(arrays),
+        scratch_shapes=[pltpu.SemaphoreType.DMA((total,))],
         cost_estimate=pl.CostEstimate(flops=0, bytes_accessed=2 * size, transcendentals=0),
         compiler_params=pltpu.CompilerParams(vmem_limit_bytes=8 * MIB),
         name="stage",
-    )(*(pltpu.with_memory_space_constraint(a, pltpu.HBM) for a in arrays))
-
-
-def near_body(first, neighbors, before, own, after, matrices, out, held):
+    )(*(pltpu.with_memory_space_constraint(a, pltpu.HBM) for a in (*indices, *arrays)))
+
+
+def near_body(place, neighbors, paired, own, inside, across, matrices, out, held):
     rows = own.shape[0]
     boxes, near, width, _ = matrices.shape
     tiles = own.shape[1] // LANES
-    for part, source in enumerate((before, own, after)):
+    bits = boxes.bit_length() - 1
+    from_across = place[2] != 0
+    for part, source in enumerate((paired, own, inside)):
         for t in range(tiles):
             tile = source[:, t * LANES : (t + 1) * LANES]
+            if part == 2:
+                tile = jnp.where(from_across, across[:, t * LANES : (t + 1) * LANES], tile)
             held[0, part * tiles + t] = tile
             held[1, part * tiles + t] = pltpu.roll(tile, LANES // 2, 1)
     low = lax.broadcasted_iota(jnp.int32, (rows, LANES), 1) < LANES // 2
-    base = first[0]
+    base, direction = place[0], place[1]
+
+    def found(n, g):
+        offset = neighbors[n, g] - base
+        slot = 1 + (offset >> bits) * direction
+        return slot * tiles + ((offset & (boxes - 1)) >> 1), offset & 1
+
     for pair in range(boxes // 2):
         sums = []
         for g in (2 * pair, 2 * pair + 1):
             sides = []
             for n in range(0, near, 2):
-                a = neighbors[n, g] - base
-                b = neighbors[n + 1, g] - base
-                lower = held[a & 1, a >> 1]
-                upper = held[1 - (b & 1), b >> 1]
+                a, a_half = found(n, g)
+                b, b_half = found(n + 1, g)
+                lower = held[a_half, a]
+                upper = held[1 - b_half, b]
                 sides.append(jnp.where(low, lower, upper))
             sums.append(
                 jnp.dot(
@@ -142,14 +148,14 @@
         out[:, pair * LANES : (pair + 1) * LANES] = joined
 
 
-def near_sums(first, neighbors, before, own, after, matrices):
+def near_sums(place, neighbors, paired, own, inside, across, matrices):
     smem = pl.BlockSpec(memory_space=pltpu.SMEM)
     vmem = pl.BlockSpec(memory_space=pltpu.VMEM)
     rows, columns = own.shape
     return pl.pallas_call(
         near_body,
         out_shape=jax.ShapeDtypeStruct(own.shape, own.dtype),
-        in_specs=[smem, smem, vmem, vmem, vmem, vmem],
+        in_specs=[smem, smem, vmem, vmem, vmem, vmem, vmem],
         out_specs=vmem,
         scratch_shapes=[pltpu.VMEM((2, 3 * columns // LANES, rows, LANES), own.dtype)],
         cost_estimate=pl.CostEstimate(
@@ -157,39 +163,61 @@
         ),
         compiler_params=pltpu.CompilerParams(vmem_limit_bytes=8 * MIB),
         name="near",
-    )(first, neighbors, before, own, after, matrices)
+    )(place, neighbors, paired, own, inside, across, matrices)
 
 
 def per_device(coefficients, factors, pattern, octree_order, panels, near_blocks, neighbors):
     boxes = pattern.shape[1]
-    col_bits = lax.axis_size("col").bit_length() - 1
+    columns = lax.axis_size("col")
+    col_bits = columns.bit_length() - 1
     row_bits = lax.axis_size("row").bit_length() - 1
     both = ("row", "col")
     count = lax.axis_size(both)
-    up = [(i, i + 1) for i in range(count - 1)]
-    down = [(j, i) for i, j in up]
+    tie = lax.optimization_barrier
+    me = lax.axis_index(both).astype(jnp.int32)
+
+    def crosses(i):
+        return (i + 1) % (columns // 2) == 0
+
+    def swaps(kept):
+        odd = [i for i in range(1, count - 1, 2) if kept(i)]
+        return [(i, i + 1) for i in odd] + [(i + 1, i) for i in odd]
+
     partner = exchange(coefficients, "col", 1 << (col_bits - 1))
-    before = lax.ppermute(panels, both, up)
-    after = lax.ppermute(panels, both, down)
-    matrices = jnp.swapaxes(factors, 2, 3)
-    blocks, matrices, pattern, octree_order = staged(
-        coefficients, matrices, pattern, octree_order
-    )
-    levels = factors.shape[0]
-    for level in range(levels):
-        if level == 0:
-            pass
-        elif level % 2 == 0:
-            partner = exchange(blocks, "col", 1 << (col_bits - 1 - level // 2))
-        else:
-            partner = exchange(blocks, "row", 1 << (row_bits - 1 - level // 2))
-        blocks = combine(
-            level, level == levels - 1, pattern, octree_order, blocks, partner, matrices
-        )
-    first = (lax.axis_index(both) * boxes - boxes).astype(jnp.int32).reshape(1)
+    paired = lax.ppermute(panels, both, [(i, i ^ 1) for i in range(count)])
+    across = lax.ppermute(panels, both, swaps(crosses))
+    half = columns // 2
+    at_edge = jnp.where(me & 1 == 1, (me + 1) % half, me % half) == 0
+    place = jnp.stack([me * boxes, 2 * (me & 1) - 1, at_edge.astype(jnp.int32)])
+    pattern, octree_order, neighbors, place, blocks, matrices = staged(
+        (pattern, octree_order, jnp.swapaxes(neighbors, 0, 1), place),
+        (coefficients, jnp.swapaxes(factors, 2, 3)),
+    )
+
+    def level(index, blocks, partner, last=False):
+        return combine(index, last, pattern, octree_order, blocks, partner, matrices)
+
+    blocks = level(0, blocks, partner)
+    partner = exchange(blocks, "row", 1 << (row_bits - 1))
+    partner, paired, across = tie((partner, paired, across))
+    blocks = level(1, blocks, partner)
+    partner = exchange(blocks, "col", 1 << (col_bits - 2))
+    blocks, panels, near_blocks = tie((blocks, panels, near_blocks))
+    (near_blocks,) = staged((), (near_blocks,))
+    partner, near_blocks = tie((partner, near_blocks))
+    inside = lax.ppermute(panels, both, swaps(lambda i: not crosses(i)))
     near_field = near_sums(
-        first, jnp.swapaxes(neighbors, 0, 1), before, panels, after, near_blocks
-    )
+        place,
+        neighbors,
+        paired,
+        panels,
+        inside,
+        across,
+        near_blocks,
+    )
+    blocks = level(2, blocks, partner)
+    partner = exchange(blocks, "row", 1 << (row_bits - 2))
+    blocks = level(3, blocks, partner, True)
     return (blocks, near_field)
 
 

time: 67.7 us -> 63.3 us (0.935)
  the two profiles are of different devices: /device:TPU:1 before, /device:TPU:24 now
where the time goes in v3:
time: 63.3 us; the launch traced here: 63 us
  starting transfers between devices  37.5 us (59%)
  waiting for transfers between devices  16 us (25%)
  Pallas kernels  8.1 us (13%)
  between operations  0.79 us (1%)
  other arithmetic  0.64 us (1%)
    ppermute x4, starting transfers between devices, exchange(): return lax.ppermute(value, axis, pairs)  31.5 us
    ppermute x4, waiting for transfers between devices, exchange(): return lax.ppermute(value, axis, pairs)  14.2 us
    pallas_call x2, Pallas kernels, staged(): pl.pallas_call(stage_body, out_shape=[pltpu.SMEM(a.shape, a.dtype) for a...  3.66 us
    ppermute x1, starting transfers between devices, per_device(): paired = lax.ppermute(panels, both, [(i, i ^ 1) for i in range(count)])  3.4 us
    pallas_call x4, Pallas kernels, combine(): pl.pallas_call(functools.partial(level_body, level, ordered), out_shape=j...  2.64 us
    ppermute x1, starting transfers between devices, per_device(): across = lax.ppermute(panels, both, swaps(crosses))  1.92 us
    pallas_call x1, Pallas kernels, near_sums(): pl.pallas_call(near_body, out_shape=jax.ShapeDtypeStruct(own.shape, own.d...  1.8 us
    ppermute x1, waiting for transfers between devices, per_device(): across = lax.ppermute(panels, both, swaps(crosses))  1.78 us
  transfers between devices with their start and end apart: 7, of which 4 were waited for; matrix products, arithmetic and copies ran while one was open for 1% of the time, Pallas kernels for 10%

profile of v3, /device:TPU:24, one launch (start us, length us, event | category | flops | bytes accessed | tf_op | source)
XLA Modules:
  0.0 63.0 jit_solution(5670440973700174815)
XLA Ops:
  0.6 15.7 %collective-permute-start = (bf16[32,2048]{1,0:T(8,128)(2,1)}, bf16[32,2048]{1,0:T(8,128)(2,1)S(1)}, u32[]{:S(2)}, u32[]{:S(2)}) collective-permute-start(bf16[32,2048]{1,0:T(8,128)(2,1)} %refs_4_.1), channel_id=1, source_target_pairs={{0,16},{1,17},{2,18},{3,19},{4,20},{5,21},{6,22},{7,23},{8,24},{9,... | collective-permute-start | bytes 393224 | tf_op jit(solution)/shard_map/ppermute | solution.py:17
  16.4 3.4 %collective-permute-start.2 = (bf16[32,2048]{1,0:T(8,128)(2,1)}, bf16[32,2048]{1,0:T(8,128)(2,1)S(1)}, u32[]{:S(2)}, u32[]{:S(2)}) collective-permute-start(bf16[32,2048]{1,0:T(8,128)(2,1)} %own), channel_id=1, source_target_pairs={{0,1},{1,0},{2,3},{3,2},{4,5},{5,4},{6,7},{7,6},{8,9},{9,8},{10,11... | collective-permute-start | bytes 393224 | tf_op jit(solution)/shard_map/ppermute | solution.py:187
  19.8 1.9 %collective-permute-start.3 = (bf16[32,2048]{1,0:T(8,128)(2,1)}, bf16[32,2048]{1,0:T(8,128)(2,1)S(1)}, u32[]{:S(2)}, u32[]{:S(2)}) collective-permute-start(bf16[32,2048]{1,0:T(8,128)(2,1)} %own), channel_id=1, source_target_pairs={{15,16},{31,32},{47,48},{63,64},{79,80},{95,96},{111,112},{127,128... | collective-permute-start | bytes 393224 | tf_op jit(solution)/shard_map/ppermute | solution.py:188
  21.7 0.6 %pad_add_fusion.refs_3_ = s32[3]{0:T(128)} fusion(s32[1]{0:T(128)} %bitcast.3, s32[1]{0:T(128)} %bitcast.2, s32[1]{0:T(128)} %bitcast.1), kind=kLoop, calls=%fused_computation | loop fusion | flops 6 | bytes 24 | tf_op jit(solution)/shard_map/stack | solution.py:191
  22.4 0.0 copy-start
  22.4 1.8 %stage.2 = (s32[4,32]{1,0:T(4,128)S(4)}, s32[32]{0:T(128)S(4)}, s32[6,32]{1,0:T(8,128)S(4)}, s32[3]{0:T(128)S(4)}, bf16[32,2048]{1,0:T(8,128)(2,1)S(1)}, /*index=5*/bf16[4,32,64,128]{3,2,1,0:T(8,128)(2,1)S(1)}) custom-call(s32[4,32]{1,0:T(4,128)} %refs_0_.1, s32[32]{0:T(128)} %refs_1_.1, s32[6,32]{1,0:T(8,128)} %bitcast.6, s32[3]{0:T(128)} %pad_add_fusion.refs_3_, ...), custom_call_target="tpu_custom_call" | custom-call | bytes 4456448 | tf_op jit(solution)/shard_map/stage/pallas_call | solution.py:96
  24.1 0.0 collective-permute-done.partner
  24.1 0.5 level0.1.own
  24.7 4.6 %collective-permute-start.1 = (bf16[32,2048]{1,0:T(8,128)(2,1)S(1)}, bf16[32,2048]{1,0:T(8,128)(2,1)S(1)}, u32[]{:S(2)}, u32[]{:S(2)}) collective-permute-start(bf16[32,2048]{1,0:T(8,128)(2,1)S(1)} %level0.1.own), channel_id=1, source_target_pairs={{0,256},{32,288},{64,320},{96,352},{128,384},{160,416},{192,448},{... | collective-permute-start | bytes 393224 | tf_op jit(solution)/shard_map/ppermute | solution.py:17
  29.3 0.0 collective-permute-done.2.paired
  29.3 1.8 %collective-permute-done.3.across = bf16[32,2048]{1,0:T(8,128)(2,1)S(1)} collective-permute-done((bf16[32,2048]{1,0:T(8,128)(2,1)}, bf16[32,2048]{1,0:T(8,128)(2,1)S(1)}, u32[]{:S(2)}, u32[]{:S(2)}) %collective-permute-start.3) | collective-permute-done | bytes 131104 | tf_op jit(solution)/shard_map/ppermute | solution.py:188
  31.1 2.5 %collective-permute-done.1.partner = bf16[32,2048]{1,0:T(8,128)(2,1)S(1)} collective-permute-done((bf16[32,2048]{1,0:T(8,128)(2,1)S(1)}, bf16[32,2048]{1,0:T(8,128)(2,1)S(1)}, u32[]{:S(2)}, u32[]{:S(2)}) %collective-permute-start.1) | collective-permute-done | bytes 131104 | tf_op jit(solution)/shard_map/ppermute | solution.py:17
  33.6 0.5 level1.1.own
  34.1 8.0 %collective-permute-start.4 = (bf16[32,2048]{1,0:T(8,128)(2,1)S(1)}, bf16[32,2048]{1,0:T(8,128)(2,1)S(1)}, u32[]{:S(2)}, u32[]{:S(2)}) collective-permute-start(bf16[32,2048]{1,0:T(8,128)(2,1)S(1)} %level1.1.own), channel_id=1, source_target_pairs={{0,8},{1,9},{2,10},{3,11},{4,12},{5,13},{6,14},{7,15},{8,0},{9,1},... | collective-permute-start | bytes 393224 | tf_op jit(solution)/shard_map/ppermute | solution.py:17
  42.1 0.0 copy-done
  42.1 0.7 %collective-permute-start.6 = (bf16[32,2048]{1,0:T(8,128)(2,1)S(1)}, bf16[32,2048]{1,0:T(8,128)(2,1)S(1)}, u32[]{:S(2)}, u32[]{:S(2)}) collective-permute-start(bf16[32,2048]{1,0:T(8,128)(2,1)S(1)} %copy-done), channel_id=1, source_target_pairs={{1,2},{3,4},{5,6},{7,8},{9,10},{11,12},{13,14},{17,18},{19,20},{21... | collective-permute-start | bytes 393224 | tf_op jit(solution)/shard_map/ppermute | solution.py:208
  42.8 1.9 %stage.3.matrices = bf16[32,6,64,64]{3,2,1,0:T(8,128)(2,1)S(1)} custom-call(bf16[32,6,64,64]{3,2,1,0:T(8,128)(2,1)} %refs_0_.2), custom_call_target="tpu_custom_call" | custom-call | bytes 3145728 | tf_op jit(solution)/shard_map/stage/pallas_call | solution.py:96
  44.7 8.3 %collective-permute-done.4.partner = bf16[32,2048]{1,0:T(8,128)(2,1)S(1)} collective-permute-done((bf16[32,2048]{1,0:T(8,128)(2,1)S(1)}, bf16[32,2048]{1,0:T(8,128)(2,1)S(1)}, u32[]{:S(2)}, u32[]{:S(2)}) %collective-permute-start.4) | collective-permute-done | bytes 131104 | tf_op jit(solution)/shard_map/ppermute | solution.py:17
  53.0 0.5 level2.1.own
  53.5 3.1 %collective-permute-start.5 = (bf16[32,2048]{1,0:T(8,128)(2,1)S(1)}, bf16[32,2048]{1,0:T(8,128)(2,1)S(1)}, u32[]{:S(2)}, u32[]{:S(2)}) collective-permute-start(bf16[32,2048]{1,0:T(8,128)(2,1)S(1)} %level2.1.own), channel_id=1, source_target_pairs={{0,128},{32,160},{64,192},{96,224},{128,0},{160,32},{192,64},{224,... | collective-permute-start | bytes 393224 | tf_op jit(solution)/shard_map/ppermute | solution.py:17
  56.7 0.0 collective-permute-done.6.inside
  56.7 1.8 %near.1 = bf16[32,2048]{1,0:T(8,128)(2,1)} custom-call(s32[3]{0:T(128)S(4)} %get-tuple-element.24.place, s32[6,32]{1,0:T(8,128)S(4)} %get-tuple-element.25.neighbors, bf16[32,2048]{1,0:T(8,128)(2,1)S(1)} %collective-permute-done.2.paired, bf16[32,2048]{1,0:T(8,128)(2,1)S(1)} %copy-done, bf16[32,2048]{1,0:T(8,128)(2,1)S(1)} %collective-permute-done.6.inside, ...), custom_call_target="tpu_custom_call" | custom-call | flops 50331648 | bytes 4194304 | tf_op jit(solution)/shard_map/near/pallas_call | solution.py:155
  58.5 3.4 %collective-permute-done.5.partner = bf16[32,2048]{1,0:T(8,128)(2,1)S(1)} collective-permute-done((bf16[32,2048]{1,0:T(8,128)(2,1)S(1)}, bf16[32,2048]{1,0:T(8,128)(2,1)S(1)}, u32[]{:S(2)}, u32[]{:S(2)}) %collective-permute-start.5) | collective-permute-done | bytes 131104 | tf_op jit(solution)/shard_map/ppermute | solution.py:17
  61.9 1.1 %level3.1 = bf16[32,2048]{1,0:T(8,128)(2,1)} custom-call(s32[4,32]{1,0:T(4,128)S(4)} %get-tuple-element.16.pattern, s32[32]{0:T(128)S(4)} %get-tuple-element.17.order, bf16[32,2048]{1,0:T(8,128)(2,1)S(1)} %level2.1.own, bf16[32,2048]{1,0:T(8,128)(2,1)S(1)} %collective-permute-done.5.partner, bf16[4,32,64,128]{3,2,1,0:T(8,128)(2,1)S(1)} %get-tuple-element.19.matrices), custom_call_target="tpu_custom_call" | custom-call | flops 16777216 | bytes 1048576 | tf_op jit(solution)/shard_map/level3/pallas_call | solution.py:64
Async XLA Ops:
  0.6 23.5 %collective-permute-start = (bf16[32,2048]{1,0:T(8,128)(2,1)}, bf16[32,2048]{1,0:T(8,128)(2,1)S(1)}, u32[]{:S(2)}, u32[]{:S(2)}) collective-permute-start(bf16[32,2048]{1,0:T(8,128)(2,1)} %refs_4_.1), channel_id=1, source_target_pairs={{0,16},{1,17},{2,18},{3,19},{4,20},{5,21},{6,22},{7,23},{8,24},{9,... | collective-permute-start | bytes 393224 | tf_op jit(solution)/shard_map/ppermute | solution.py:17
  16.4 12.9 %collective-permute-start.2 = (bf16[32,2048]{1,0:T(8,128)(2,1)}, bf16[32,2048]{1,0:T(8,128)(2,1)S(1)}, u32[]{:S(2)}, u32[]{:S(2)}) collective-permute-start(bf16[32,2048]{1,0:T(8,128)(2,1)} %own), channel_id=1, source_target_pairs={{0,1},{1,0},{2,3},{3,2},{4,5},{5,4},{6,7},{7,6},{8,9},{9,8},{10,11... | collective-permute-start | bytes 393224 | tf_op jit(solution)/shard_map/ppermute | solution.py:187
  19.8 11.3 %collective-permute-start.3 = (bf16[32,2048]{1,0:T(8,128)(2,1)}, bf16[32,2048]{1,0:T(8,128)(2,1)S(1)}, u32[]{:S(2)}, u32[]{:S(2)}) collective-permute-start(bf16[32,2048]{1,0:T(8,128)(2,1)} %own), channel_id=1, source_target_pairs={{15,16},{31,32},{47,48},{63,64},{79,80},{95,96},{111,112},{127,128... | collective-permute-start | bytes 393224 | tf_op jit(solution)/shard_map/ppermute | solution.py:188
  22.4 19.8 %copy-start = (bf16[32,2048]{1,0:T(8,128)(2,1)S(1)}, bf16[32,2048]{1,0:T(8,128)(2,1)}, u32[]{:S(2)}) copy-start(bf16[32,2048]{1,0:T(8,128)(2,1)} %own) | copy-start | bytes 393220
  24.7 9.0 %collective-permute-start.1 = (bf16[32,2048]{1,0:T(8,128)(2,1)S(1)}, bf16[32,2048]{1,0:T(8,128)(2,1)S(1)}, u32[]{:S(2)}, u32[]{:S(2)}) collective-permute-start(bf16[32,2048]{1,0:T(8,128)(2,1)S(1)} %level0.1.own), channel_id=1, source_target_pairs={{0,256},{32,288},{64,320},{96,352},{128,384},{160,416},{192,448},{... | collective-permute-start | bytes 393224 | tf_op jit(solution)/shard_map/ppermute | solution.py:17
  34.1 18.9 %collective-permute-start.4 = (bf16[32,2048]{1,0:T(8,128)(2,1)S(1)}, bf16[32,2048]{1,0:T(8,128)(2,1)S(1)}, u32[]{:S(2)}, u32[]{:S(2)}) collective-permute-start(bf16[32,2048]{1,0:T(8,128)(2,1)S(1)} %level1.1.own), channel_id=1, source_target_pairs={{0,8},{1,9},{2,10},{3,11},{4,12},{5,13},{6,14},{7,15},{8,0},{9,1},... | collective-permute-start | bytes 393224 | tf_op jit(solution)/shard_map/ppermute | solution.py:17
  42.1 14.5 %collective-permute-start.6 = (bf16[32,2048]{1,0:T(8,128)(2,1)S(1)}, bf16[32,2048]{1,0:T(8,128)(2,1)S(1)}, u32[]{:S(2)}, u32[]{:S(2)}) collective-permute-start(bf16[32,2048]{1,0:T(8,128)(2,1)S(1)} %copy-done), channel_id=1, source_target_pairs={{1,2},{3,4},{5,6},{7,8},{9,10},{11,12},{13,14},{17,18},{19,20},{21... | collective-permute-start | bytes 393224 | tf_op jit(solution)/shard_map/ppermute | solution.py:208
  53.5 8.4 %collective-permute-start.5 = (bf16[32,2048]{1,0:T(8,128)(2,1)S(1)}, bf16[32,2048]{1,0:T(8,128)(2,1)S(1)}, u32[]{:S(2)}, u32[]{:S(2)}) collective-permute-start(bf16[32,2048]{1,0:T(8,128)(2,1)S(1)} %level2.1.own), channel_id=1, source_target_pairs={{0,128},{32,160},{64,192},{96,224},{128,0},{160,32},{192,64},{224,... | collective-permute-start | bytes 393224 | tf_op jit(solution)/shard_map/ppermute | solution.py:17

commit v4 on v3

--- a/solution.py
+++ b/solution.py
@@ -106,22 +106,21 @@
     )(*(pltpu.with_memory_space_constraint(a, pltpu.HBM) for a in (*indices, *arrays)))
 
 
-def near_body(place, neighbors, paired, own, inside, across, matrices, out, held):
+def near_body(neighbors, paired, own, inside, across, matrices, out, held):
     rows = own.shape[0]
     boxes, near, width, _ = matrices.shape
     tiles = own.shape[1] // LANES
     bits = boxes.bit_length() - 1
-    from_across = place[2] != 0
+    base = neighbors[0, 0]
+    direction = 2 * ((base >> bits) & 1) - 1
     for part, source in enumerate((paired, own, inside)):
         for t in range(tiles):
             tile = source[:, t * LANES : (t + 1) * LANES]
             if part == 2:
-                tile = jnp.where(from_across, across[:, t * LANES : (t + 1) * LANES], tile)
+                tile = tile + across[:, t * LANES : (t + 1) * LANES]
             held[0, part * tiles + t] = tile
             held[1, part * tiles + t] = pltpu.roll(tile, LANES // 2, 1)
     low = lax.broadcasted_iota(jnp.int32, (rows, LANES), 1) < LANES // 2
-    base, direction = place[0], place[1]
-
     def found(n, g):
         offset = neighbors[n, g] - base
         slot = 1 + (offset >> bits) * direction
@@ -148,14 +147,14 @@
         out[:, pair * LANES : (pair + 1) * LANES] = joined
 
 
-def near_sums(place, neighbors, paired, own, inside, across, matrices):
+def near_sums(neighbors, paired, own, inside, across, matrices):
     smem = pl.BlockSpec(memory_space=pltpu.SMEM)
     vmem = pl.BlockSpec(memory_space=pltpu.VMEM)
     rows, columns = own.shape
     return pl.pallas_call(
         near_body,
         out_shape=jax.ShapeDtypeStruct(own.shape, own.dtype),
-        in_specs=[smem, smem, vmem, vmem, vmem, vmem, vmem],
+        in_specs=[smem, vmem, vmem, vmem, vmem, vmem],
         out_specs=vmem,
         scratch_shapes=[pltpu.VMEM((2, 3 * columns // LANES, rows, LANES), own.dtype)],
         cost_estimate=pl.CostEstimate(
@@ -163,7 +162,7 @@
         ),
         compiler_params=pltpu.CompilerParams(vmem_limit_bytes=8 * MIB),
         name="near",
-    )(place, neighbors, paired, own, inside, across, matrices)
+    )(neighbors, paired, own, inside, across, matrices)
 
 
 def per_device(coefficients, factors, pattern, octree_order, panels, near_blocks, neighbors):
@@ -174,7 +173,6 @@
     both = ("row", "col")
     count = lax.axis_size(both)
     tie = lax.optimization_barrier
-    me = lax.axis_index(both).astype(jnp.int32)
 
     def crosses(i):
         return (i + 1) % (columns // 2) == 0
@@ -184,14 +182,10 @@
         return [(i, i + 1) for i in odd] + [(i + 1, i) for i in odd]
 
     partner = exchange(coefficients, "col", 1 << (col_bits - 1))
-    paired = lax.ppermute(panels, both, [(i, i ^ 1) for i in range(count)])
     across = lax.ppermute(panels, both, swaps(crosses))
-    half = columns // 2
-    at_edge = jnp.where(me & 1 == 1, (me + 1) % half, me % half) == 0
-    place = jnp.stack([me * boxes, 2 * (me & 1) - 1, at_edge.astype(jnp.int32)])
-    pattern, octree_order, neighbors, place, blocks, matrices = staged(
-        (pattern, octree_order, jnp.swapaxes(neighbors, 0, 1), place),
-        (coefficients, jnp.swapaxes(factors, 2, 3)),
+    pattern, octree_order, neighbors, blocks, matrices, near_blocks = staged(
+        (pattern, octree_order, jnp.swapaxes(neighbors, 0, 1)),
+        (coefficients, jnp.swapaxes(factors, 2, 3), near_blocks),
     )
 
     def level(index, blocks, partner, last=False):
@@ -199,15 +193,13 @@
 
     blocks = level(0, blocks, partner)
     partner = exchange(blocks, "row", 1 << (row_bits - 1))
-    partner, paired, across = tie((partner, paired, across))
+    partner, across = tie((partner, across))
     blocks = level(1, blocks, partner)
     partner = exchange(blocks, "col", 1 << (col_bits - 2))
-    blocks, panels, near_blocks = tie((blocks, panels, near_blocks))
-    (near_blocks,) = staged((), (near_blocks,))
-    partner, near_blocks = tie((partner, near_blocks))
+    blocks, panels = tie((blocks, panels))
+    paired = lax.ppermute(panels, both, [(i, i ^ 1) for i in range(count)])
     inside = lax.ppermute(panels, both, swaps(lambda i: not crosses(i)))
     near_field = near_sums(
-        place,
         neighbors,
         paired,
         panels,

time: 63.3 us -> 62.2 us (0.983)
  starting transfers between devices: 37.5 us -> 40 us
  waiting for transfers between devices: 16 us -> 14.1 us
  Pallas kernels: 8.1 us -> 7.09 us
  other arithmetic: 0.64 us -> 0 us
    ppermute x4, waiting for transfers between devices: 14.2 us -> 9.46 us  [exchange(): return lax.ppermute(value, axis, pairs)]
    ppermute x1, waiting for transfers between devices: 1.78 us -> 4.6 us  [per_device(): across = lax.ppermute(panels, both, swaps(crosses))]
    ppermute x4, starting transfers between devices: 31.5 us -> 33.7 us  [exchange(): return lax.ppermute(value, axis, pairs)]
    pallas_call x2 -> x1, Pallas kernels: 3.66 us -> 2.65 us  [staged(): pl.pallas_call(stage_body, out_shape=[pltpu.SMEM(a.shape, a.dtype) for a...]
    another operation x1 -> x0, other arithmetic: 0.64 us -> none  [per_device(): place = jnp.stack([me * boxes, 2 * (me & 1) - 1, at_edge.astype(jnp.int32)])]
  transfers between devices with their start and end apart: 7 -> 7, of which waited for: 4 -> 4; matrix products, arithmetic and copies ran while one was open for 1% -> 0% of each run, Pallas kernels for 10% -> 9%
where the time goes in v4:
time: 62.2 us; the launch traced here: 61.9 us
  starting transfers between devices  40 us (64%)
  waiting for transfers between devices  14.1 us (23%)
  Pallas kernels  7.09 us (11%)
  between operations  0.76 us (1%)
    ppermute x4, starting transfers between devices, exchange(): return lax.ppermute(value, axis, pairs)  33.7 us
    ppermute x4, waiting for transfers between devices, exchange(): return lax.ppermute(value, axis, pairs)  9.46 us
    ppermute x1, waiting for transfers between devices, per_device(): across = lax.ppermute(panels, both, swaps(crosses))  4.6 us
    ppermute x1, starting transfers between devices, per_device(): paired = lax.ppermute(panels, both, [(i, i ^ 1) for i in range(count)])  3.36 us
    pallas_call x1, Pallas kernels, staged(): pl.pallas_call(stage_body, out_shape=[pltpu.SMEM(a.shape, a.dtype) for a...  2.65 us
    pallas_call x4, Pallas kernels, combine(): pl.pallas_call(functools.partial(level_body, level, ordered), out_shape=j...  2.63 us
    ppermute x1, starting transfers between devices, per_device(): across = lax.ppermute(panels, both, swaps(crosses))  2.29 us
    pallas_call x1, Pallas kernels, near_sums(): pl.pallas_call(near_body, out_shape=jax.ShapeDtypeStruct(own.shape, own.d...  1.8 us
  transfers between devices with their start and end apart: 7, of which 4 were waited for; matrix products, arithmetic and copies ran while one was open for 0% of the time, Pallas kernels for 9%

profile of v4, /device:TPU:24, one launch (start us, length us, event | category | flops | bytes accessed | tf_op | source)
XLA Modules:
  0.0 61.9 jit_solution(15476536674917837286)
XLA Ops:
  0.6 15.7 %collective-permute-start = (bf16[32,2048]{1,0:T(8,128)(2,1)}, bf16[32,2048]{1,0:T(8,128)(2,1)S(1)}, u32[]{:S(2)}, u32[]{:S(2)}) collective-permute-start(bf16[32,2048]{1,0:T(8,128)(2,1)} %refs_3_.1), channel_id=1, source_target_pairs={{0,16},{1,17},{2,18},{3,19},{4,20},{5,21},{6,22},{7,23},{8,24},{9,... | collective-permute-start | bytes 393224 | tf_op jit(solution)/shard_map/ppermute | solution.py:17
  16.4 2.3 %collective-permute-start.2 = (bf16[32,2048]{1,0:T(8,128)(2,1)}, bf16[32,2048]{1,0:T(8,128)(2,1)S(1)}, u32[]{:S(2)}, u32[]{:S(2)}) collective-permute-start(bf16[32,2048]{1,0:T(8,128)(2,1)} %own), channel_id=1, source_target_pairs={{15,16},{31,32},{47,48},{63,64},{79,80},{95,96},{111,112},{127,128... | collective-permute-start | bytes 393224 | tf_op jit(solution)/shard_map/ppermute | solution.py:185
  18.7 2.7 %stage.1 = (s32[4,32]{1,0:T(4,128)S(4)}, s32[32]{0:T(128)S(4)}, s32[6,32]{1,0:T(8,128)S(4)}, bf16[32,2048]{1,0:T(8,128)(2,1)S(1)}, bf16[4,32,64,128]{3,2,1,0:T(8...) custom-call(s32[4,32]{1,0:T(4,128)} %refs_0_.1, s32[32]{0:T(128)} %refs_1_.1, s32[6,32]{1,0:T(8,128)} %bitcast.3, ...), custom_call_target="tpu_custom_call" | custom-call | bytes 7602176 | tf_op jit(solution)/shard_map/stage/pallas_call | solution.py:96
  21.3 0.0 copy-start
  21.3 0.0 collective-permute-done.partner
  21.3 0.5 level0.1.own
  21.9 4.6 %collective-permute-start.1 = (bf16[32,2048]{1,0:T(8,128)(2,1)S(1)}, bf16[32,2048]{1,0:T(8,128)(2,1)S(1)}, u32[]{:S(2)}, u32[]{:S(2)}) collective-permute-start(bf16[32,2048]{1,0:T(8,128)(2,1)S(1)} %level0.1.own), channel_id=1, source_target_pairs={{0,256},{32,288},{64,320},{96,352},{128,384},{160,416},{192,448},{... | collective-permute-start | bytes 393224 | tf_op jit(solution)/shard_map/ppermute | solution.py:17
  26.5 4.6 %collective-permute-done.2.across = bf16[32,2048]{1,0:T(8,128)(2,1)S(1)} collective-permute-done((bf16[32,2048]{1,0:T(8,128)(2,1)}, bf16[32,2048]{1,0:T(8,128)(2,1)S(1)}, u32[]{:S(2)}, u32[]{:S(2)}) %collective-permute-start.2) | collective-permute-done | bytes 131104 | tf_op jit(solution)/shard_map/ppermute | solution.py:185
  31.1 0.3 collective-permute-done.1.partner
  31.4 0.5 level1.1.own
  31.9 10.2 %collective-permute-start.3 = (bf16[32,2048]{1,0:T(8,128)(2,1)S(1)}, bf16[32,2048]{1,0:T(8,128)(2,1)S(1)}, u32[]{:S(2)}, u32[]{:S(2)}) collective-permute-start(bf16[32,2048]{1,0:T(8,128)(2,1)S(1)} %level1.1.own), channel_id=1, source_target_pairs={{0,8},{1,9},{2,10},{3,11},{4,12},{5,13},{6,14},{7,15},{8,0},{9,1},... | collective-permute-start | bytes 393224 | tf_op jit(solution)/shard_map/ppermute | solution.py:17
  42.1 0.0 copy-done
  42.1 3.4 %collective-permute-start.5 = (bf16[32,2048]{1,0:T(8,128)(2,1)S(1)}, bf16[32,2048]{1,0:T(8,128)(2,1)S(1)}, u32[]{:S(2)}, u32[]{:S(2)}) collective-permute-start(bf16[32,2048]{1,0:T(8,128)(2,1)S(1)} %copy-done), channel_id=1, source_target_pairs={{0,1},{1,0},{2,3},{3,2},{4,5},{5,4},{6,7},{7,6},{8,9},{9,8},{10,11... | collective-permute-start | bytes 393224 | tf_op jit(solution)/shard_map/ppermute | solution.py:200
  45.5 0.7 %collective-permute-start.6 = (bf16[32,2048]{1,0:T(8,128)(2,1)S(1)}, bf16[32,2048]{1,0:T(8,128)(2,1)S(1)}, u32[]{:S(2)}, u32[]{:S(2)}) collective-permute-start(bf16[32,2048]{1,0:T(8,128)(2,1)S(1)} %copy-done), channel_id=1, source_target_pairs={{1,2},{3,4},{5,6},{7,8},{9,10},{11,12},{13,14},{17,18},{19,20},{21... | collective-permute-start | bytes 393224 | tf_op jit(solution)/shard_map/ppermute | solution.py:201
  46.2 5.7 %collective-permute-done.3.partner = bf16[32,2048]{1,0:T(8,128)(2,1)S(1)} collective-permute-done((bf16[32,2048]{1,0:T(8,128)(2,1)S(1)}, bf16[32,2048]{1,0:T(8,128)(2,1)S(1)}, u32[]{:S(2)}, u32[]{:S(2)}) %collective-permute-start.3) | collective-permute-done | bytes 131104 | tf_op jit(solution)/shard_map/ppermute | solution.py:17
  51.9 0.5 level2.1.own
  52.4 3.2 %collective-permute-start.4 = (bf16[32,2048]{1,0:T(8,128)(2,1)S(1)}, bf16[32,2048]{1,0:T(8,128)(2,1)S(1)}, u32[]{:S(2)}, u32[]{:S(2)}) collective-permute-start(bf16[32,2048]{1,0:T(8,128)(2,1)S(1)} %level2.1.own), channel_id=1, source_target_pairs={{0,128},{32,160},{64,192},{96,224},{128,0},{160,32},{192,64},{224,... | collective-permute-start | bytes 393224 | tf_op jit(solution)/shard_map/ppermute | solution.py:17
  55.6 0.0 collective-permute-done.5.paired
  55.6 0.0 collective-permute-done.6.inside
  55.6 1.8 %near.1 = bf16[32,2048]{1,0:T(8,128)(2,1)} custom-call(s32[6,32]{1,0:T(8,128)S(4)} %get-tuple-element.18.neighbors, bf16[32,2048]{1,0:T(8,128)(2,1)S(1)} %collective-permute-done.5.paired, bf16[32,2048]{1,0:T(8,128)(2,1)S(1)} %copy-done, bf16[32,2048]{1,0:T(8,128)(2,1)S(1)} %collective-permute-done.6.inside, ...), custom_call_target="tpu_custom_call" | custom-call | flops 50331648 | bytes 4194304 | tf_op jit(solution)/shard_map/near/pallas_call | solution.py:154
  57.4 3.4 %collective-permute-done.4.partner = bf16[32,2048]{1,0:T(8,128)(2,1)S(1)} collective-permute-done((bf16[32,2048]{1,0:T(8,128)(2,1)S(1)}, bf16[32,2048]{1,0:T(8,128)(2,1)S(1)}, u32[]{:S(2)}, u32[]{:S(2)}) %collective-permute-start.4) | collective-permute-done | bytes 131104 | tf_op jit(solution)/shard_map/ppermute | solution.py:17
  60.8 1.1 %level3.1 = bf16[32,2048]{1,0:T(8,128)(2,1)} custom-call(s32[4,32]{1,0:T(4,128)S(4)} %get-tuple-element.12.pattern, s32[32]{0:T(128)S(4)} %get-tuple-element.13.order, bf16[32,2048]{1,0:T(8,128)(2,1)S(1)} %level2.1.own, bf16[32,2048]{1,0:T(8,128)(2,1)S(1)} %collective-permute-done.4.partner, bf16[4,32,64,128]{3,2,1,0:T(8,128)(2,1)S(1)} %get-tuple-element.15.matrices), custom_call_target="tpu_custom_call" | custom-call | flops 16777216 | bytes 1048576 | tf_op jit(solution)/shard_map/level3/pallas_call | solution.py:64
Async XLA Ops:
  0.6 20.7 %collective-permute-start = (bf16[32,2048]{1,0:T(8,128)(2,1)}, bf16[32,2048]{1,0:T(8,128)(2,1)S(1)}, u32[]{:S(2)}, u32[]{:S(2)}) collective-permute-start(bf16[32,2048]{1,0:T(8,128)(2,1)} %refs_3_.1), channel_id=1, source_target_pairs={{0,16},{1,17},{2,18},{3,19},{4,20},{5,21},{6,22},{7,23},{8,24},{9,... | collective-permute-start | bytes 393224 | tf_op jit(solution)/shard_map/ppermute | solution.py:17
  16.4 14.7 %collective-permute-start.2 = (bf16[32,2048]{1,0:T(8,128)(2,1)}, bf16[32,2048]{1,0:T(8,128)(2,1)S(1)}, u32[]{:S(2)}, u32[]{:S(2)}) collective-permute-start(bf16[32,2048]{1,0:T(8,128)(2,1)} %own), channel_id=1, source_target_pairs={{15,16},{31,32},{47,48},{63,64},{79,80},{95,96},{111,112},{127,128... | collective-permute-start | bytes 393224 | tf_op jit(solution)/shard_map/ppermute | solution.py:185
  21.3 20.8 %copy-start = (bf16[32,2048]{1,0:T(8,128)(2,1)S(1)}, bf16[32,2048]{1,0:T(8,128)(2,1)}, u32[]{:S(2)}) copy-start(bf16[32,2048]{1,0:T(8,128)(2,1)} %own) | copy-start | bytes 393220
  21.9 9.6 %collective-permute-start.1 = (bf16[32,2048]{1,0:T(8,128)(2,1)S(1)}, bf16[32,2048]{1,0:T(8,128)(2,1)S(1)}, u32[]{:S(2)}, u32[]{:S(2)}) collective-permute-start(bf16[32,2048]{1,0:T(8,128)(2,1)S(1)} %level0.1.own), channel_id=1, source_target_pairs={{0,256},{32,288},{64,320},{96,352},{128,384},{160,416},{192,448},{... | collective-permute-start | bytes 393224 | tf_op jit(solution)/shard_map/ppermute | solution.py:17
  31.9 20.0 %collective-permute-start.3 = (bf16[32,2048]{1,0:T(8,128)(2,1)S(1)}, bf16[32,2048]{1,0:T(8,128)(2,1)S(1)}, u32[]{:S(2)}, u32[]{:S(2)}) collective-permute-start(bf16[32,2048]{1,0:T(8,128)(2,1)S(1)} %level1.1.own), channel_id=1, source_target_pairs={{0,8},{1,9},{2,10},{3,11},{4,12},{5,13},{6,14},{7,15},{8,0},{9,1},... | collective-permute-start | bytes 393224 | tf_op jit(solution)/shard_map/ppermute | solution.py:17
  42.1 13.5 %collective-permute-start.5 = (bf16[32,2048]{1,0:T(8,128)(2,1)S(1)}, bf16[32,2048]{1,0:T(8,128)(2,1)S(1)}, u32[]{:S(2)}, u32[]{:S(2)}) collective-permute-start(bf16[32,2048]{1,0:T(8,128)(2,1)S(1)} %copy-done), channel_id=1, source_target_pairs={{0,1},{1,0},{2,3},{3,2},{4,5},{5,4},{6,7},{7,6},{8,9},{9,8},{10,11... | collective-permute-start | bytes 393224 | tf_op jit(solution)/shard_map/ppermute | solution.py:200
  45.5 10.1 %collective-permute-start.6 = (bf16[32,2048]{1,0:T(8,128)(2,1)S(1)}, bf16[32,2048]{1,0:T(8,128)(2,1)S(1)}, u32[]{:S(2)}, u32[]{:S(2)}) collective-permute-start(bf16[32,2048]{1,0:T(8,128)(2,1)S(1)} %copy-done), channel_id=1, source_target_pairs={{1,2},{3,4},{5,6},{7,8},{9,10},{11,12},{13,14},{17,18},{19,20},{21... | collective-permute-start | bytes 393224 | tf_op jit(solution)/shard_map/ppermute | solution.py:201
  52.4 8.4 %collective-permute-start.4 = (bf16[32,2048]{1,0:T(8,128)(2,1)S(1)}, bf16[32,2048]{1,0:T(8,128)(2,1)S(1)}, u32[]{:S(2)}, u32[]{:S(2)}) collective-permute-start(bf16[32,2048]{1,0:T(8,128)(2,1)S(1)} %level2.1.own), channel_id=1, source_target_pairs={{0,128},{32,160},{64,192},{96,224},{128,0},{160,32},{192,64},{224,... | collective-permute-start | bytes 393224 | tf_op jit(solution)/shard_map/ppermute | solution.py:17

commit v5 on v4

--- a/solution.py
+++ b/solution.py
@@ -17,6 +17,11 @@
     return lax.ppermute(value, axis, pairs)
 
 
+def exchange_pairs(value, axis, mask):
+    pairs = [[i, i ^ mask] for i in range(lax.axis_size(axis)) if not i & mask]
+    return lax.all_gather(value, axis, axis_index_groups=pairs)
+
+
 def tile_of(ref, box):
     start = pl.multiple_of((box >> 1) * LANES, LANES)
     return ref[:, pl.ds(start, LANES)]
@@ -28,7 +33,9 @@
     return pltpu.roll(tile, shift, 1)
 
 
-def level_body(level, ordered, pattern, order, own, partner, matrices, out):
+def level_body(level, ordered, bit, pattern, order, neighbors, own, partner, matrices, out):
+    if bit is not None:
+        partner = partner.at[1 - ((neighbors[0, 0] >> bit) & 1)]
     rows = own.shape[0]
     boxes = matrices.shape[1]
     low = lax.broadcasted_iota(jnp.int32, (rows, LANES), 1) < LANES // 2
@@ -57,21 +64,21 @@
         out[:, pair * LANES : (pair + 1) * LANES] = joined.astype(out.dtype)
 
 
-def combine(level, ordered, pattern, order, own, partner, matrices):
+def combine(level, ordered, bit, pattern, order, neighbors, own, partner, matrices):
     depth = matrices.shape[3]
     smem = pl.BlockSpec(memory_space=pltpu.SMEM)
     vmem = pl.BlockSpec(memory_space=pltpu.VMEM)
     return pl.pallas_call(
-        functools.partial(level_body, level, ordered),
+        functools.partial(level_body, level, ordered, bit),
         out_shape=jax.ShapeDtypeStruct(own.shape, own.dtype),
-        in_specs=[smem, smem, vmem, vmem, vmem],
+        in_specs=[smem, smem, smem, vmem, vmem, vmem],
         out_specs=vmem,
         cost_estimate=pl.CostEstimate(
             flops=2 * own.size * depth, bytes_accessed=1 << 20, transcendentals=0
         ),
         compiler_params=pltpu.CompilerParams(vmem_limit_bytes=4 * MIB),
         name=f"level{level}",
-    )(pattern, order, own, partner, matrices)
+    )(pattern, order, neighbors, own, partner, matrices)
 
 
 def stage_body(*refs):
@@ -147,22 +154,29 @@
         out[:, pair * LANES : (pair + 1) * LANES] = joined
 
 
-def near_sums(neighbors, paired, own, inside, across, matrices):
+def last_body(level, bit, pattern, order, neighbors, own, gathered, matrices, *refs):
+    paired, panels, inside, across, near_blocks, far_out, near_out, held = refs
+    level_body(level, True, bit, pattern, order, neighbors, own, gathered, matrices, far_out)
+    near_body(neighbors, paired, panels, inside, across, near_blocks, near_out, held)
+
+
+def last_and_near(level, bit, indices, own, gathered, matrices, halos, near_blocks):
     smem = pl.BlockSpec(memory_space=pltpu.SMEM)
     vmem = pl.BlockSpec(memory_space=pltpu.VMEM)
     rows, columns = own.shape
+    out = jax.ShapeDtypeStruct(own.shape, own.dtype)
     return pl.pallas_call(
-        near_body,
-        out_shape=jax.ShapeDtypeStruct(own.shape, own.dtype),
-        in_specs=[smem, vmem, vmem, vmem, vmem, vmem],
-        out_specs=vmem,
+        functools.partial(last_body, level, bit),
+        out_shape=[out, out],
+        in_specs=[smem] * 3 + [vmem] * 8,
+        out_specs=[vmem, vmem],
         scratch_shapes=[pltpu.VMEM((2, 3 * columns // LANES, rows, LANES), own.dtype)],
         cost_estimate=pl.CostEstimate(
-            flops=2 * own.size * 384, bytes_accessed=4 << 20, transcendentals=0
+            flops=2 * own.size * 512, bytes_accessed=5 << 20, transcendentals=0
         ),
         compiler_params=pltpu.CompilerParams(vmem_limit_bytes=8 * MIB),
-        name="near",
-    )(neighbors, paired, own, inside, across, matrices)
+        name="last",
+    )(*indices, own, gathered, matrices, *halos, near_blocks)
 
 
 def per_device(coefficients, factors, pattern, octree_order, panels, near_blocks, neighbors):
@@ -188,29 +202,32 @@
         (coefficients, jnp.swapaxes(factors, 2, 3), near_blocks),
     )
 
-    def level(index, blocks, partner, last=False):
-        return combine(index, last, pattern, octree_order, blocks, partner, matrices)
+    def level(index, blocks, partner, last=False, bit=None):
+        return combine(
+            index, last, bit, pattern, octree_order, neighbors, blocks, partner, matrices
+        )
 
     blocks = level(0, blocks, partner)
-    partner = exchange(blocks, "row", 1 << (row_bits - 1))
-    partner, across = tie((partner, across))
-    blocks = level(1, blocks, partner)
+    gathered = exchange_pairs(blocks, "row", 1 << (row_bits - 1))
+    gathered, across = tie((gathered, across))
+    own_bit = boxes.bit_length() - 1 + col_bits
+    blocks = level(1, blocks, gathered, bit=own_bit + row_bits - 1)
     partner = exchange(blocks, "col", 1 << (col_bits - 2))
     blocks, panels = tie((blocks, panels))
     paired = lax.ppermute(panels, both, [(i, i ^ 1) for i in range(count)])
     inside = lax.ppermute(panels, both, swaps(lambda i: not crosses(i)))
-    near_field = near_sums(
-        neighbors,
-        paired,
-        panels,
-        inside,
-        across,
+    blocks = level(2, blocks, partner)
+    gathered = exchange_pairs(blocks, "row", 1 << (row_bits - 2))
+    return last_and_near(
+        3,
+        own_bit + row_bits - 2,
+        (pattern, octree_order, neighbors),
+        blocks,
+        gathered,
+        matrices,
+        (paired, panels, inside, across),
         near_blocks,
     )
-    blocks = level(2, blocks, partner)
-    partner = exchange(blocks, "row", 1 << (row_bits - 2))
-    blocks = level(3, blocks, partner, True)
-    return (blocks, near_field)
 
 
 def solution(mesh):

time: 62.2 us -> 62.3 us (level)
  blocking collectives: 0 us -> 15.5 us
  starting transfers between devices: 40 us -> 32.6 us
  waiting for transfers between devices: 14.1 us -> 6.97 us
  Pallas kernels: 7.09 us -> 6.23 us
    all_gather x0 -> x2, blocking collectives: none -> 15.5 us  [exchange_pairs(): return lax.all_gather(value, axis, axis_index_groups=pairs)]
    ppermute x4 -> x2, starting transfers between devices: 33.7 us -> 25 us  [exchange(): return lax.ppermute(value, axis, pairs)]
    ppermute x1, waiting for transfers between devices: 4.6 us -> 0.88 us  [per_device(): across = lax.ppermute(panels, both, swaps(crosses))]
    ppermute x4 -> x2, waiting for transfers between devices: 9.46 us -> 6.09 us  [exchange(): return lax.ppermute(value, axis, pairs)]
    ppermute x1, starting transfers between devices: 3.36 us -> 4.61 us  [per_device(): paired = lax.ppermute(panels, both, [(i, i ^ 1) for i in range(count)])]
    pallas_call x5 -> x4, Pallas kernels: 4.43 us -> 3.58 us  [the longest x1 2.08 us: last_and_near(): pl.pallas_call(functools.partial(last_body, level, bit), out_shape=[out,...]
  transfers between devices with their start and end apart: 7 -> 5, of which waited for: 4 -> 2; matrix products, arithmetic and copies ran while one was open for 0% -> 0% of each run, Pallas kernels for 9% -> 6%
where the time goes in v5:
time: 62.3 us; the launch traced here: 62 us
  starting transfers between devices  32.6 us (52%)
  blocking collectives  15.5 us (25%)
  waiting for transfers between devices  6.97 us (11%)
  Pallas kernels  6.23 us (10%)
  between operations  0.73 us (1%)
    ppermute x2, starting transfers between devices, exchange(): return lax.ppermute(value, axis, pairs)  25 us
    all_gather x2, blocking collectives, exchange_pairs(): return lax.all_gather(value, axis, axis_index_groups=pairs)  15.5 us
    ppermute x2, waiting for transfers between devices, exchange(): return lax.ppermute(value, axis, pairs)  6.09 us
    ppermute x1, starting transfers between devices, per_device(): paired = lax.ppermute(panels, both, [(i, i ^ 1) for i in range(count)])  4.61 us
    pallas_call x1, Pallas kernels, staged(): pl.pallas_call(stage_body, out_shape=[pltpu.SMEM(a.shape, a.dtype) for a...  2.65 us
    ppermute x1, starting transfers between devices, per_device(): across = lax.ppermute(panels, both, swaps(crosses))  2.29 us
    pallas_call x1, Pallas kernels, last_and_near(): pl.pallas_call(functools.partial(last_body, level, bit), out_shape=[out,...  2.08 us
    pallas_call x3, Pallas kernels, combine(): pl.pallas_call(functools.partial(level_body, level, ordered, bit), out_sh...  1.5 us
  transfers between devices with their start and end apart: 5, of which 2 were waited for; matrix products, arithmetic and copies ran while one was open for 0% of the time, Pallas kernels for 6%

profile of v5, /device:TPU:24, one launch (start us, length us, event | category | flops | bytes accessed | tf_op | source)
XLA Modules:
  0.0 62.0 jit_solution(9122973557046633969)
XLA Ops:
  0.6 15.7 %collective-permute-start = (bf16[32,2048]{1,0:T(8,128)(2,1)}, bf16[32,2048]{1,0:T(8,128)(2,1)S(1)}, u32[]{:S(2)}, u32[]{:S(2)}) collective-permute-start(bf16[32,2048]{1,0:T(8,128)(2,1)} %refs_3_.1), channel_id=1, source_target_pairs={{0,16},{1,17},{2,18},{3,19},{4,20},{5,21},{6,22},{7,23},{8,24},{9,... | collective-permute-start | bytes 393224 | tf_op jit(solution)/shard_map/ppermute | solution.py:17
  16.4 2.3 %collective-permute-start.1 = (bf16[32,2048]{1,0:T(8,128)(2,1)}, bf16[32,2048]{1,0:T(8,128)(2,1)S(1)}, u32[]{:S(2)}, u32[]{:S(2)}) collective-permute-start(bf16[32,2048]{1,0:T(8,128)(2,1)} %refs_1_.2), channel_id=1, source_target_pairs={{15,16},{31,32},{47,48},{63,64},{79,80},{95,96},{111,112},{127,128... | collective-permute-start | bytes 393224 | tf_op jit(solution)/shard_map/ppermute | solution.py:199
  18.7 2.7 %stage.1 = (s32[4,32]{1,0:T(4,128)S(4)}, s32[32]{0:T(128)S(4)}, s32[6,32]{1,0:T(8,128)S(4)}, bf16[32,2048]{1,0:T(8,128)(2,1)S(1)}, bf16[4,32,64,128]{3,2,1,0:T(8...) custom-call(s32[4,32]{1,0:T(4,128)} %refs_0_.1, s32[32]{0:T(128)} %refs_1_.1, s32[6,32]{1,0:T(8,128)} %bitcast.7, ...), custom_call_target="tpu_custom_call" | custom-call | bytes 7602176 | tf_op jit(solution)/shard_map/stage/pallas_call | solution.py:103
  21.3 0.0 copy-start
  21.3 0.0 collective-permute-done.partner
  21.3 0.5 level0.1.own
  21.9 8.4 %all-gather = bf16[64,2048]{1,0:T(8,128)(2,1)S(1)} all-gather(bf16[32,2048]{1,0:T(8,128)(2,1)S(1)} %level0.1.own), channel_id=2, replica_groups={{0,256},{32,288},{64,320},{96,352},{128,384},{160,416},{192,448},{224,4..., dimensions={0}, use_global_device_ids=true | all-gather | bytes 393216 | tf_op jit(solution)/shard_map/all_gather | solution.py:22
  30.2 0.9 %collective-permute-done.1.refs_3_ = bf16[32,2048]{1,0:T(8,128)(2,1)S(1)} collective-permute-done((bf16[32,2048]{1,0:T(8,128)(2,1)}, bf16[32,2048]{1,0:T(8,128)(2,1)S(1)}, u32[]{:S(2)}, u32[]{:S(2)}) %collective-permute-start.1) | collective-permute-done | bytes 131104 | tf_op jit(solution)/shard_map/ppermute | solution.py:199
  31.1 0.5 level1.1.own
  31.6 9.3 %collective-permute-start.2 = (bf16[32,2048]{1,0:T(8,128)(2,1)S(1)}, bf16[32,2048]{1,0:T(8,128)(2,1)S(1)}, u32[]{:S(2)}, u32[]{:S(2)}) collective-permute-start(bf16[32,2048]{1,0:T(8,128)(2,1)S(1)} %level1.1.own), channel_id=1, source_target_pairs={{0,8},{1,9},{2,10},{3,11},{4,12},{5,13},{6,14},{7,15},{8,0},{9,1},... | collective-permute-start | bytes 393224 | tf_op jit(solution)/shard_map/ppermute | solution.py:17
  40.9 0.0 copy-done
  40.9 0.7 %collective-permute-start.4 = (bf16[32,2048]{1,0:T(8,128)(2,1)S(1)}, bf16[32,2048]{1,0:T(8,128)(2,1)S(1)}, u32[]{:S(2)}, u32[]{:S(2)}) collective-permute-start(bf16[32,2048]{1,0:T(8,128)(2,1)S(1)} %copy-done), channel_id=1, source_target_pairs={{1,2},{3,4},{5,6},{7,8},{9,10},{11,12},{13,14},{17,18},{19,20},{21... | collective-permute-start | bytes 393224 | tf_op jit(solution)/shard_map/ppermute | solution.py:218
  41.6 4.6 %collective-permute-start.3 = (bf16[32,2048]{1,0:T(8,128)(2,1)S(1)}, bf16[32,2048]{1,0:T(8,128)(2,1)S(1)}, u32[]{:S(2)}, u32[]{:S(2)}) collective-permute-start(bf16[32,2048]{1,0:T(8,128)(2,1)S(1)} %copy-done), channel_id=1, source_target_pairs={{0,1},{1,0},{2,3},{3,2},{4,5},{5,4},{6,7},{7,6},{8,9},{9,8},{10,11... | collective-permute-start | bytes 393224 | tf_op jit(solution)/shard_map/ppermute | solution.py:217
  46.2 6.1 %collective-permute-done.2.partner = bf16[32,2048]{1,0:T(8,128)(2,1)S(1)} collective-permute-done((bf16[32,2048]{1,0:T(8,128)(2,1)S(1)}, bf16[32,2048]{1,0:T(8,128)(2,1)S(1)}, u32[]{:S(2)}, u32[]{:S(2)}) %collective-permute-start.2) | collective-permute-done | bytes 131104 | tf_op jit(solution)/shard_map/ppermute | solution.py:17
  52.3 0.5 level2.1.own
  52.8 7.1 %all-gather.1 = bf16[64,2048]{1,0:T(8,128)(2,1)S(1)} all-gather(bf16[32,2048]{1,0:T(8,128)(2,1)S(1)} %level2.1.own), channel_id=3, replica_groups={{0,128},{32,160},{64,192},{96,224},{256,384},{288,416},{320,448},{352,4..., dimensions={0}, use_global_device_ids=true | all-gather | bytes 393216 | tf_op jit(solution)/shard_map/all_gather | solution.py:22
  60.0 0.0 collective-permute-done.4.refs_2_
  60.0 0.0 collective-permute-done.3.refs_0_
  60.0 2.1 %last.1 = (bf16[32,2048]{1,0:T(8,128)(2,1)}, bf16[32,2048]{1,0:T(8,128)(2,1)}) custom-call(s32[4,32]{1,0:T(4,128)S(4)} %get-tuple-element.12.pattern, s32[32]{0:T(128)S(4)} %get-tuple-element.13.order, s32[6,32]{1,0:T(8,128)S(4)} %get-tuple-element.14.neighbors, bf16[32,2048]{1,0:T(8,128)(2,1)S(1)} %level2.1.own, bf16[2,32,2048]{2,1,0:T(8,128)(2,1)S(1)} %bitcast.5, ...), custom_call_target="tpu_custom_call" | custom-call | flops 67108864 | bytes 5242880 | tf_op jit(solution)/shard_map/last/pallas_call | solution.py:168
Async XLA Ops:
  0.6 20.7 %collective-permute-start = (bf16[32,2048]{1,0:T(8,128)(2,1)}, bf16[32,2048]{1,0:T(8,128)(2,1)S(1)}, u32[]{:S(2)}, u32[]{:S(2)}) collective-permute-start(bf16[32,2048]{1,0:T(8,128)(2,1)} %refs_3_.1), channel_id=1, source_target_pairs={{0,16},{1,17},{2,18},{3,19},{4,20},{5,21},{6,22},{7,23},{8,24},{9,... | collective-permute-start | bytes 393224 | tf_op jit(solution)/shard_map/ppermute | solution.py:17
  16.4 14.7 %collective-permute-start.1 = (bf16[32,2048]{1,0:T(8,128)(2,1)}, bf16[32,2048]{1,0:T(8,128)(2,1)S(1)}, u32[]{:S(2)}, u32[]{:S(2)}) collective-permute-start(bf16[32,2048]{1,0:T(8,128)(2,1)} %refs_1_.2), channel_id=1, source_target_pairs={{15,16},{31,32},{47,48},{63,64},{79,80},{95,96},{111,112},{127,128... | collective-permute-start | bytes 393224 | tf_op jit(solution)/shard_map/ppermute | solution.py:199
  21.3 19.6 %copy-start = (bf16[32,2048]{1,0:T(8,128)(2,1)S(1)}, bf16[32,2048]{1,0:T(8,128)(2,1)}, u32[]{:S(2)}) copy-start(bf16[32,2048]{1,0:T(8,128)(2,1)} %refs_1_.2) | copy-start | bytes 393220
  31.6 20.7 %collective-permute-start.2 = (bf16[32,2048]{1,0:T(8,128)(2,1)S(1)}, bf16[32,2048]{1,0:T(8,128)(2,1)S(1)}, u32[]{:S(2)}, u32[]{:S(2)}) collective-permute-start(bf16[32,2048]{1,0:T(8,128)(2,1)S(1)} %level1.1.own), channel_id=1, source_target_pairs={{0,8},{1,9},{2,10},{3,11},{4,12},{5,13},{6,14},{7,15},{8,0},{9,1},... | collective-permute-start | bytes 393224 | tf_op jit(solution)/shard_map/ppermute | solution.py:17
  40.9 19.0 %collective-permute-start.4 = (bf16[32,2048]{1,0:T(8,128)(2,1)S(1)}, bf16[32,2048]{1,0:T(8,128)(2,1)S(1)}, u32[]{:S(2)}, u32[]{:S(2)}) collective-permute-start(bf16[32,2048]{1,0:T(8,128)(2,1)S(1)} %copy-done), channel_id=1, source_target_pairs={{1,2},{3,4},{5,6},{7,8},{9,10},{11,12},{13,14},{17,18},{19,20},{21... | collective-permute-start | bytes 393224 | tf_op jit(solution)/shard_map/ppermute | solution.py:218
  41.6 18.4 %collective-permute-start.3 = (bf16[32,2048]{1,0:T(8,128)(2,1)S(1)}, bf16[32,2048]{1,0:T(8,128)(2,1)S(1)}, u32[]{:S(2)}, u32[]{:S(2)}) collective-permute-start(bf16[32,2048]{1,0:T(8,128)(2,1)S(1)} %copy-done), channel_id=1, source_target_pairs={{0,1},{1,0},{2,3},{3,2},{4,5},{5,4},{6,7},{7,6},{8,9},{9,8},{10,11... | collective-permute-start | bytes 393224 | tf_op jit(solution)/shard_map/ppermute | solution.py:217

commit v6 on v5

--- a/solution.py
+++ b/solution.py
@@ -113,7 +113,7 @@
     )(*(pltpu.with_memory_space_constraint(a, pltpu.HBM) for a in (*indices, *arrays)))
 
 
-def near_body(neighbors, paired, own, inside, across, matrices, out, held):
+def near_body(neighbors, paired, own, inside, wrapped, across, matrices, out, held):
     rows = own.shape[0]
     boxes, near, width, _ = matrices.shape
     tiles = own.shape[1] // LANES
@@ -124,6 +124,7 @@
         for t in range(tiles):
             tile = source[:, t * LANES : (t + 1) * LANES]
             if part == 2:
+                tile = tile + wrapped[:, t * LANES : (t + 1) * LANES]
                 tile = tile + across[:, t * LANES : (t + 1) * LANES]
             held[0, part * tiles + t] = tile
             held[1, part * tiles + t] = pltpu.roll(tile, LANES // 2, 1)
@@ -155,9 +156,11 @@
 
 
 def last_body(level, bit, pattern, order, neighbors, own, gathered, matrices, *refs):
-    paired, panels, inside, across, near_blocks, far_out, near_out, held = refs
+    paired, panels, inside, wrapped, across, near_blocks, far_out, near_out, held = refs
     level_body(level, True, bit, pattern, order, neighbors, own, gathered, matrices, far_out)
-    near_body(neighbors, paired, panels, inside, across, near_blocks, near_out, held)
+    near_body(
+        neighbors, paired, panels, inside, wrapped, across, near_blocks, near_out, held
+    )
 
 
 def last_and_near(level, bit, indices, own, gathered, matrices, halos, near_blocks):
@@ -168,7 +171,7 @@
     return pl.pallas_call(
         functools.partial(last_body, level, bit),
         out_shape=[out, out],
-        in_specs=[smem] * 3 + [vmem] * 8,
+        in_specs=[smem] * 3 + [vmem] * 9,
         out_specs=[vmem, vmem],
         scratch_shapes=[pltpu.VMEM((2, 3 * columns // LANES, rows, LANES), own.dtype)],
         cost_estimate=pl.CostEstimate(
@@ -191,12 +194,15 @@
     def crosses(i):
         return (i + 1) % (columns // 2) == 0
 
+    def wraps(i):
+        return (i + 1) % (2 * columns) == columns
+
     def swaps(kept):
         odd = [i for i in range(1, count - 1, 2) if kept(i)]
         return [(i, i + 1) for i in odd] + [(i + 1, i) for i in odd]
 
     partner = exchange(coefficients, "col", 1 << (col_bits - 1))
-    across = lax.ppermute(panels, both, swaps(crosses))
+    wrapped = lax.ppermute(panels, both, swaps(wraps))
     pattern, octree_order, neighbors, blocks, matrices, near_blocks = staged(
         (pattern, octree_order, jnp.swapaxes(neighbors, 0, 1)),
         (coefficients, jnp.swapaxes(factors, 2, 3), near_blocks),
@@ -209,13 +215,14 @@
 
     blocks = level(0, blocks, partner)
     gathered = exchange_pairs(blocks, "row", 1 << (row_bits - 1))
-    gathered, across = tie((gathered, across))
+    gathered, wrapped = tie((gathered, wrapped))
     own_bit = boxes.bit_length() - 1 + col_bits
     blocks = level(1, blocks, gathered, bit=own_bit + row_bits - 1)
     partner = exchange(blocks, "col", 1 << (col_bits - 2))
     blocks, panels = tie((blocks, panels))
     paired = lax.ppermute(panels, both, [(i, i ^ 1) for i in range(count)])
     inside = lax.ppermute(panels, both, swaps(lambda i: not crosses(i)))
+    across = lax.ppermute(panels, both, swaps(lambda i: crosses(i) and not wraps(i)))
     blocks = level(2, blocks, partner)
     gathered = exchange_pairs(blocks, "row", 1 << (row_bits - 2))
     return last_and_near(
@@ -225,7 +232,7 @@
         blocks,
         gathered,
         matrices,
-        (paired, panels, inside, across),
+        (paired, panels, inside, wrapped, across),
         near_blocks,
     )
 

time: 62.3 us -> 60.6 us (0.973)
  waiting for transfers between devices: 6.97 us -> 3.79 us
  starting transfers between devices: 32.6 us -> 34.1 us
    ppermute x2, starting transfers between devices: 25 us -> 27.5 us  [exchange(): return lax.ppermute(value, axis, pairs)]
    ppermute x2, waiting for transfers between devices: 6.09 us -> 3.78 us  [exchange(): return lax.ppermute(value, axis, pairs)]
    ppermute x1, starting transfers between devices: 4.61 us -> 3.36 us  [per_device(): paired = lax.ppermute(panels, both, [(i, i ^ 1) for i in range(count)])]
    ppermute x1 -> x2, waiting for transfers between devices: 0.88 us -> 0.01 us  [the longest x1 0.01 us: per_device(): wrapped = lax.ppermute(panels, both, swaps(wraps))]
    ppermute x1 -> x2, starting transfers between devices: 2.29 us -> 2.59 us  [the longest x1 1.92 us: per_device(): lax.ppermute(panels, both, swaps(lambda i: crosses(i) and (not wraps(i))))]
  transfers between devices with their start and end apart: 5 -> 6, of which waited for: 2 -> 2; matrix products, arithmetic and copies ran while one was open for 0% -> 0% of each run, Pallas kernels for 6% -> 6%
where the time goes in v6:
time: 60.6 us; the launch traced here: 59.8 us
  starting transfers between devices  34.1 us (56%)
  blocking collectives  14.9 us (25%)
  Pallas kernels  6.26 us (10%)
  waiting for transfers between devices  3.79 us (6%)
  between operations  0.73 us (1%)
    ppermute x2, starting transfers between devices, exchange(): return lax.ppermute(value, axis, pairs)  27.5 us
    all_gather x2, blocking collectives, exchange_pairs(): return lax.all_gather(value, axis, axis_index_groups=pairs)  14.9 us
    ppermute x2, waiting for transfers between devices, exchange(): return lax.ppermute(value, axis, pairs)  3.78 us
    ppermute x1, starting transfers between devices, per_device(): paired = lax.ppermute(panels, both, [(i, i ^ 1) for i in range(count)])  3.36 us
    pallas_call x1, Pallas kernels, staged(): pl.pallas_call(stage_body, out_shape=[pltpu.SMEM(a.shape, a.dtype) for a...  2.65 us
    pallas_call x1, Pallas kernels, last_and_near(): pl.pallas_call(functools.partial(last_body, level, bit), out_shape=[out,...  2.11 us
    ppermute x1, starting transfers between devices, per_device(): lax.ppermute(panels, both, swaps(lambda i: crosses(i) and (not wraps(i))))  1.92 us
    pallas_call x3, Pallas kernels, combine(): pl.pallas_call(functools.partial(level_body, level, ordered, bit), out_sh...  1.49 us
  transfers between devices with their start and end apart: 6, of which 2 were waited for; matrix products, arithmetic and copies ran while one was open for 0% of the time, Pallas kernels for 6%

profile of v6, /device:TPU:24, one launch (start us, length us, event | category | flops | bytes accessed | tf_op | source)
XLA Modules:
  0.0 59.8 jit_solution(9019894432239377959)
XLA Ops:
  0.6 15.7 %collective-permute-start = (bf16[32,2048]{1,0:T(8,128)(2,1)}, bf16[32,2048]{1,0:T(8,128)(2,1)S(1)}, u32[]{:S(2)}, u32[]{:S(2)}) collective-permute-start(bf16[32,2048]{1,0:T(8,128)(2,1)} %refs_3_.1), channel_id=1, source_target_pairs={{0,16},{1,17},{2,18},{3,19},{4,20},{5,21},{6,22},{7,23},{8,24},{9,... | collective-permute-start | bytes 393224 | tf_op jit(solution)/shard_map/ppermute | solution.py:17
  16.4 0.7 %collective-permute-start.1 = (bf16[32,2048]{1,0:T(8,128)(2,1)}, bf16[32,2048]{1,0:T(8,128)(2,1)S(1)}, u32[]{:S(2)}, u32[]{:S(2)}) collective-permute-start(bf16[32,2048]{1,0:T(8,128)(2,1)} %refs_1_.2), channel_id=1, source_target_pairs={{31,32},{95,96},{159,160},{223,224},{287,288},{351,352},{415,416},... | collective-permute-start | bytes 393224 | tf_op jit(solution)/shard_map/ppermute | solution.py:205
  17.0 2.7 %stage.1 = (s32[4,32]{1,0:T(4,128)S(4)}, s32[32]{0:T(128)S(4)}, s32[6,32]{1,0:T(8,128)S(4)}, bf16[32,2048]{1,0:T(8,128)(2,1)S(1)}, bf16[4,32,64,128]{3,2,1,0:T(8...) custom-call(s32[4,32]{1,0:T(4,128)} %refs_0_.1, s32[32]{0:T(128)} %refs_1_.1, s32[6,32]{1,0:T(8,128)} %bitcast.7, ...), custom_call_target="tpu_custom_call" | custom-call | bytes 7602176 | tf_op jit(solution)/shard_map/stage/pallas_call | solution.py:103
  19.7 0.0 copy-start
  19.7 0.6 %collective-permute-done.partner = bf16[32,2048]{1,0:T(8,128)(2,1)S(1)} collective-permute-done((bf16[32,2048]{1,0:T(8,128)(2,1)}, bf16[32,2048]{1,0:T(8,128)(2,1)S(1)}, u32[]{:S(2)}, u32[]{:S(2)}) %collective-permute-start) | collective-permute-done | bytes 131104 | tf_op jit(solution)/shard_map/ppermute | solution.py:17
  20.4 0.5 level0.1.own
  20.9 7.8 %all-gather = bf16[64,2048]{1,0:T(8,128)(2,1)S(1)} all-gather(bf16[32,2048]{1,0:T(8,128)(2,1)S(1)} %level0.1.own), channel_id=2, replica_groups={{0,256},{32,288},{64,320},{96,352},{128,384},{160,416},{192,448},{224,4..., dimensions={0}, use_global_device_ids=true | all-gather | bytes 393216 | tf_op jit(solution)/shard_map/all_gather | solution.py:22
  28.7 0.0 collective-permute-done.1.refs_3_
  28.7 0.5 level1.1.own
  29.2 11.7 %collective-permute-start.2 = (bf16[32,2048]{1,0:T(8,128)(2,1)S(1)}, bf16[32,2048]{1,0:T(8,128)(2,1)S(1)}, u32[]{:S(2)}, u32[]{:S(2)}) collective-permute-start(bf16[32,2048]{1,0:T(8,128)(2,1)S(1)} %level1.1.own), channel_id=1, source_target_pairs={{0,8},{1,9},{2,10},{3,11},{4,12},{5,13},{6,14},{7,15},{8,0},{9,1},... | collective-permute-start | bytes 393224 | tf_op jit(solution)/shard_map/ppermute | solution.py:17
  40.9 0.0 copy-done
  40.9 1.9 %collective-permute-start.5 = (bf16[32,2048]{1,0:T(8,128)(2,1)S(1)}, bf16[32,2048]{1,0:T(8,128)(2,1)S(1)}, u32[]{:S(2)}, u32[]{:S(2)}) collective-permute-start(bf16[32,2048]{1,0:T(8,128)(2,1)S(1)} %copy-done), channel_id=1, source_target_pairs={{15,16},{47,48},{63,64},{79,80},{111,112},{127,128},{143,144},{175... | collective-permute-start | bytes 393224 | tf_op jit(solution)/shard_map/ppermute | solution.py:225
  42.8 0.7 %collective-permute-start.4 = (bf16[32,2048]{1,0:T(8,128)(2,1)S(1)}, bf16[32,2048]{1,0:T(8,128)(2,1)S(1)}, u32[]{:S(2)}, u32[]{:S(2)}) collective-permute-start(bf16[32,2048]{1,0:T(8,128)(2,1)S(1)} %copy-done), channel_id=1, source_target_pairs={{1,2},{3,4},{5,6},{7,8},{9,10},{11,12},{13,14},{17,18},{19,20},{21... | collective-permute-start | bytes 393224 | tf_op jit(solution)/shard_map/ppermute | solution.py:224
  43.5 3.4 %collective-permute-start.3 = (bf16[32,2048]{1,0:T(8,128)(2,1)S(1)}, bf16[32,2048]{1,0:T(8,128)(2,1)S(1)}, u32[]{:S(2)}, u32[]{:S(2)}) collective-permute-start(bf16[32,2048]{1,0:T(8,128)(2,1)S(1)} %copy-done), channel_id=1, source_target_pairs={{0,1},{1,0},{2,3},{3,2},{4,5},{5,4},{6,7},{7,6},{8,9},{9,8},{10,11... | collective-permute-start | bytes 393224 | tf_op jit(solution)/shard_map/ppermute | solution.py:223
  46.9 3.1 %collective-permute-done.2.partner = bf16[32,2048]{1,0:T(8,128)(2,1)S(1)} collective-permute-done((bf16[32,2048]{1,0:T(8,128)(2,1)S(1)}, bf16[32,2048]{1,0:T(8,128)(2,1)S(1)}, u32[]{:S(2)}, u32[]{:S(2)}) %collective-permute-start.2) | collective-permute-done | bytes 131104 | tf_op jit(solution)/shard_map/ppermute | solution.py:17
  50.0 0.5 level2.1.own
  50.5 7.1 %all-gather.1 = bf16[64,2048]{1,0:T(8,128)(2,1)S(1)} all-gather(bf16[32,2048]{1,0:T(8,128)(2,1)S(1)} %level2.1.own), channel_id=3, replica_groups={{0,128},{32,160},{64,192},{96,224},{256,384},{288,416},{320,448},{352,4..., dimensions={0}, use_global_device_ids=true | all-gather | bytes 393216 | tf_op jit(solution)/shard_map/all_gather | solution.py:22
  57.7 0.0 collective-permute-done.5.refs_4_
  57.7 0.0 collective-permute-done.4.refs_2_
  57.7 0.0 collective-permute-done.3.refs_0_
  57.7 2.1 %last.1 = (bf16[32,2048]{1,0:T(8,128)(2,1)}, bf16[32,2048]{1,0:T(8,128)(2,1)}) custom-call(s32[4,32]{1,0:T(4,128)S(4)} %get-tuple-element.12.pattern, s32[32]{0:T(128)S(4)} %get-tuple-element.13.order, s32[6,32]{1,0:T(8,128)S(4)} %get-tuple-element.14.neighbors, bf16[32,2048]{1,0:T(8,128)(2,1)S(1)} %level2.1.own, bf16[2,32,2048]{2,1,0:T(8,128)(2,1)S(1)} %bitcast.5, ...), custom_call_target="tpu_custom_call" | custom-call | flops 67108864 | bytes 5242880 | tf_op jit(solution)/shard_map/last/pallas_call | solution.py:171
Async XLA Ops:
  0.6 19.7 %collective-permute-start = (bf16[32,2048]{1,0:T(8,128)(2,1)}, bf16[32,2048]{1,0:T(8,128)(2,1)S(1)}, u32[]{:S(2)}, u32[]{:S(2)}) collective-permute-start(bf16[32,2048]{1,0:T(8,128)(2,1)} %refs_3_.1), channel_id=1, source_target_pairs={{0,16},{1,17},{2,18},{3,19},{4,20},{5,21},{6,22},{7,23},{8,24},{9,... | collective-permute-start | bytes 393224 | tf_op jit(solution)/shard_map/ppermute | solution.py:17
  16.4 12.3 %collective-permute-start.1 = (bf16[32,2048]{1,0:T(8,128)(2,1)}, bf16[32,2048]{1,0:T(8,128)(2,1)S(1)}, u32[]{:S(2)}, u32[]{:S(2)}) collective-permute-start(bf16[32,2048]{1,0:T(8,128)(2,1)} %refs_1_.2), channel_id=1, source_target_pairs={{31,32},{95,96},{159,160},{223,224},{287,288},{351,352},{415,416},... | collective-permute-start | bytes 393224 | tf_op jit(solution)/shard_map/ppermute | solution.py:205
  19.7 21.2 %copy-start = (bf16[32,2048]{1,0:T(8,128)(2,1)S(1)}, bf16[32,2048]{1,0:T(8,128)(2,1)}, u32[]{:S(2)}) copy-start(bf16[32,2048]{1,0:T(8,128)(2,1)} %refs_1_.2) | copy-start | bytes 393220
  29.2 20.9 %collective-permute-start.2 = (bf16[32,2048]{1,0:T(8,128)(2,1)S(1)}, bf16[32,2048]{1,0:T(8,128)(2,1)S(1)}, u32[]{:S(2)}, u32[]{:S(2)}) collective-permute-start(bf16[32,2048]{1,0:T(8,128)(2,1)S(1)} %level1.1.own), channel_id=1, source_target_pairs={{0,8},{1,9},{2,10},{3,11},{4,12},{5,13},{6,14},{7,15},{8,0},{9,1},... | collective-permute-start | bytes 393224 | tf_op jit(solution)/shard_map/ppermute | solution.py:17
  40.9 16.8 %collective-permute-start.5 = (bf16[32,2048]{1,0:T(8,128)(2,1)S(1)}, bf16[32,2048]{1,0:T(8,128)(2,1)S(1)}, u32[]{:S(2)}, u32[]{:S(2)}) collective-permute-start(bf16[32,2048]{1,0:T(8,128)(2,1)S(1)} %copy-done), channel_id=1, source_target_pairs={{15,16},{47,48},{63,64},{79,80},{111,112},{127,128},{143,144},{175... | collective-permute-start | bytes 393224 | tf_op jit(solution)/shard_map/ppermute | solution.py:225
  42.8 14.8 %collective-permute-start.4 = (bf16[32,2048]{1,0:T(8,128)(2,1)S(1)}, bf16[32,2048]{1,0:T(8,128)(2,1)S(1)}, u32[]{:S(2)}, u32[]{:S(2)}) collective-permute-start(bf16[32,2048]{1,0:T(8,128)(2,1)S(1)} %copy-done), channel_id=1, source_target_pairs={{1,2},{3,4},{5,6},{7,8},{9,10},{11,12},{13,14},{17,18},{19,20},{21... | collective-permute-start | bytes 393224 | tf_op jit(solution)/shard_map/ppermute | solution.py:224
  43.5 14.2 %collective-permute-start.3 = (bf16[32,2048]{1,0:T(8,128)(2,1)S(1)}, bf16[32,2048]{1,0:T(8,128)(2,1)S(1)}, u32[]{:S(2)}, u32[]{:S(2)}) collective-permute-start(bf16[32,2048]{1,0:T(8,128)(2,1)S(1)} %copy-done), channel_id=1, source_target_pairs={{0,1},{1,0},{2,3},{3,2},{4,5},{5,4},{6,7},{7,6},{8,9},{9,8},{10,11... | collective-permute-start | bytes 393224 | tf_op jit(solution)/shard_map/ppermute | solution.py:223

commit v7 on v6

--- a/solution.py
+++ b/solution.py
@@ -113,7 +113,7 @@
     )(*(pltpu.with_memory_space_constraint(a, pltpu.HBM) for a in (*indices, *arrays)))
 
 
-def near_body(neighbors, paired, own, inside, wrapped, across, matrices, out, held):
+def near_body(neighbors, early, paired, own, inside, wrapped, across, matrices, out, held):
     rows = own.shape[0]
     boxes, near, width, _ = matrices.shape
     tiles = own.shape[1] // LANES
@@ -123,6 +123,8 @@
     for part, source in enumerate((paired, own, inside)):
         for t in range(tiles):
             tile = source[:, t * LANES : (t + 1) * LANES]
+            if part == 0:
+                tile = tile + early[:, t * LANES : (t + 1) * LANES]
             if part == 2:
                 tile = tile + wrapped[:, t * LANES : (t + 1) * LANES]
                 tile = tile + across[:, t * LANES : (t + 1) * LANES]
@@ -156,10 +158,10 @@
 
 
 def last_body(level, bit, pattern, order, neighbors, own, gathered, matrices, *refs):
-    paired, panels, inside, wrapped, across, near_blocks, far_out, near_out, held = refs
+    early, paired, panels, inside, wrapped, across, near_blocks, far_out, near_out, held = refs
     level_body(level, True, bit, pattern, order, neighbors, own, gathered, matrices, far_out)
     near_body(
-        neighbors, paired, panels, inside, wrapped, across, near_blocks, near_out, held
+        neighbors, early, paired, panels, inside, wrapped, across, near_blocks, near_out, held
     )
 
 
@@ -171,7 +173,7 @@
     return pl.pallas_call(
         functools.partial(last_body, level, bit),
         out_shape=[out, out],
-        in_specs=[smem] * 3 + [vmem] * 9,
+        in_specs=[smem] * 3 + [vmem] * 10,
         out_specs=[vmem, vmem],
         scratch_shapes=[pltpu.VMEM((2, 3 * columns // LANES, rows, LANES), own.dtype)],
         cost_estimate=pl.CostEstimate(
@@ -203,6 +205,11 @@
 
     partner = exchange(coefficients, "col", 1 << (col_bits - 1))
     wrapped = lax.ppermute(panels, both, swaps(wraps))
+
+    def waits(i):
+        return i % columns >= columns // 2 or i % columns // 2 in (1, 4, 6)
+
+    early = lax.ppermute(panels, both, [(i, i ^ 1) for i in range(count) if waits(i)])
     pattern, octree_order, neighbors, blocks, matrices, near_blocks = staged(
         (pattern, octree_order, jnp.swapaxes(neighbors, 0, 1)),
         (coefficients, jnp.swapaxes(factors, 2, 3), near_blocks),
@@ -215,12 +222,12 @@
 
     blocks = level(0, blocks, partner)
     gathered = exchange_pairs(blocks, "row", 1 << (row_bits - 1))
-    gathered, wrapped = tie((gathered, wrapped))
+    gathered, wrapped, early = tie((gathered, wrapped, early))
     own_bit = boxes.bit_length() - 1 + col_bits
     blocks = level(1, blocks, gathered, bit=own_bit + row_bits - 1)
     partner = exchange(blocks, "col", 1 << (col_bits - 2))
     blocks, panels = tie((blocks, panels))
-    paired = lax.ppermute(panels, both, [(i, i ^ 1) for i in range(count)])
+    paired = lax.ppermute(panels, both, [(i, i ^ 1) for i in range(count) if not waits(i)])
     inside = lax.ppermute(panels, both, swaps(lambda i: not crosses(i)))
     across = lax.ppermute(panels, both, swaps(lambda i: crosses(i) and not wraps(i)))
     blocks = level(2, blocks, partner)
@@ -232,7 +239,7 @@
         blocks,
         gathered,
         matrices,
-        (paired, panels, inside, wrapped, across),
+        (early, paired, panels, inside, wrapped, across),
         near_blocks,
     )
 

time: 60.6 us -> 60.6 us (level)
  starting transfers between devices: 34.1 us -> 35.3 us
  waiting for transfers between devices: 3.79 us -> 3.13 us
    ppermute x1 -> x2, starting transfers between devices: 3.36 us -> 4.03 us  [the longest x1 3.36 us: per_device(): lax.ppermute(panels, both, [(i, i ^ 1) for i in range(count) if not waits...]
    ppermute x2, waiting for transfers between devices: 3.78 us -> 3.11 us  [exchange(): return lax.ppermute(value, axis, pairs)]
    all_gather x2, blocking collectives: 14.9 us -> 14.3 us  [exchange_pairs(): return lax.all_gather(value, axis, axis_index_groups=pairs)]
  transfers between devices with their start and end apart: 6 -> 7, of which waited for: 2 -> 1; matrix products, arithmetic and copies ran while one was open for 0% -> 0% of each run, Pallas kernels for 6% -> 6%
where the time goes in v7:
time: 60.6 us; the launch traced here: 59.8 us
  starting transfers between devices  35.3 us (58%)
  blocking collectives  14.3 us (24%)
  Pallas kernels  6.25 us (10%)
  waiting for transfers between devices  3.13 us (5%)
  between operations  0.75 us (1%)
    ppermute x2, starting transfers between devices, exchange(): return lax.ppermute(value, axis, pairs)  28.1 us
    all_gather x2, blocking collectives, exchange_pairs(): return lax.all_gather(value, axis, axis_index_groups=pairs)  14.3 us
    ppermute x1, starting transfers between devices, per_device(): lax.ppermute(panels, both, [(i, i ^ 1) for i in range(count) if not waits...  3.36 us
    ppermute x2, waiting for transfers between devices, exchange(): return lax.ppermute(value, axis, pairs)  3.11 us
    pallas_call x1, Pallas kernels, staged(): pl.pallas_call(stage_body, out_shape=[pltpu.SMEM(a.shape, a.dtype) for a...  2.65 us
    pallas_call x1, Pallas kernels, last_and_near(): pl.pallas_call(functools.partial(last_body, level, bit), out_shape=[out,...  2.09 us
    ppermute x1, starting transfers between devices, per_device(): lax.ppermute(panels, both, swaps(lambda i: crosses(i) and (not wraps(i))))  1.92 us
    pallas_call x3, Pallas kernels, combine(): pl.pallas_call(functools.partial(level_body, level, ordered, bit), out_sh...  1.5 us
  transfers between devices with their start and end apart: 7, of which 1 were waited for; matrix products, arithmetic and copies ran while one was open for 0% of the time, Pallas kernels for 6%

profile of v7, /device:TPU:24, one launch (start us, length us, event | category | flops | bytes accessed | tf_op | source)
XLA Modules:
  0.0 59.8 jit_solution(11685676504284370844)
XLA Ops:
  0.6 15.7 %collective-permute-start = (bf16[32,2048]{1,0:T(8,128)(2,1)}, bf16[32,2048]{1,0:T(8,128)(2,1)S(1)}, u32[]{:S(2)}, u32[]{:S(2)}) collective-permute-start(bf16[32,2048]{1,0:T(8,128)(2,1)} %refs_3_.1), channel_id=1, source_target_pairs={{0,16},{1,17},{2,18},{3,19},{4,20},{5,21},{6,22},{7,23},{8,24},{9,... | collective-permute-start | bytes 393224 | tf_op jit(solution)/shard_map/ppermute | solution.py:17
  16.4 0.7 %collective-permute-start.1 = (bf16[32,2048]{1,0:T(8,128)(2,1)}, bf16[32,2048]{1,0:T(8,128)(2,1)S(1)}, u32[]{:S(2)}, u32[]{:S(2)}) collective-permute-start(bf16[32,2048]{1,0:T(8,128)(2,1)} %refs_2_), channel_id=1, source_target_pairs={{31,32},{95,96},{159,160},{223,224},{287,288},{351,352},{415,416},... | collective-permute-start | bytes 393224 | tf_op jit(solution)/shard_map/ppermute | solution.py:207
  17.0 0.7 %collective-permute-start.2 = (bf16[32,2048]{1,0:T(8,128)(2,1)}, bf16[32,2048]{1,0:T(8,128)(2,1)S(1)}, u32[]{:S(2)}, u32[]{:S(2)}) collective-permute-start(bf16[32,2048]{1,0:T(8,128)(2,1)} %refs_2_), channel_id=1, source_target_pairs={{2,3},{3,2},{8,9},{9,8},{12,13},{13,12},{16,17},{17,16},{18,19},{1... | collective-permute-start | bytes 393224 | tf_op jit(solution)/shard_map/ppermute | solution.py:212
  17.7 2.7 %stage.1 = (s32[4,32]{1,0:T(4,128)S(4)}, s32[32]{0:T(128)S(4)}, s32[6,32]{1,0:T(8,128)S(4)}, bf16[32,2048]{1,0:T(8,128)(2,1)S(1)}, bf16[4,32,64,128]{3,2,1,0:T(8...) custom-call(s32[4,32]{1,0:T(4,128)} %refs_0_.1, s32[32]{0:T(128)} %refs_1_.1, s32[6,32]{1,0:T(8,128)} %bitcast.7, ...), custom_call_target="tpu_custom_call" | custom-call | bytes 7602176 | tf_op jit(solution)/shard_map/stage/pallas_call | solution.py:103
  20.4 0.0 copy-start
  20.4 0.0 collective-permute-done.partner
  20.4 0.5 level0.1.own
  20.9 7.1 %all-gather = bf16[64,2048]{1,0:T(8,128)(2,1)S(1)} all-gather(bf16[32,2048]{1,0:T(8,128)(2,1)S(1)} %level0.1.own), channel_id=2, replica_groups={{0,256},{32,288},{64,320},{96,352},{128,384},{160,416},{192,448},{224,4..., dimensions={0}, use_global_device_ids=true | all-gather | bytes 393216 | tf_op jit(solution)/shard_map/all_gather | solution.py:22
  28.1 0.0 collective-permute-done.1.refs_4_
  28.1 0.0 collective-permute-done.2.refs_0_
  28.1 0.5 level1.1.own
  28.6 12.3 %collective-permute-start.3 = (bf16[32,2048]{1,0:T(8,128)(2,1)S(1)}, bf16[32,2048]{1,0:T(8,128)(2,1)S(1)}, u32[]{:S(2)}, u32[]{:S(2)}) collective-permute-start(bf16[32,2048]{1,0:T(8,128)(2,1)S(1)} %level1.1.own), channel_id=1, source_target_pairs={{0,8},{1,9},{2,10},{3,11},{4,12},{5,13},{6,14},{7,15},{8,0},{9,1},... | collective-permute-start | bytes 393224 | tf_op jit(solution)/shard_map/ppermute | solution.py:17
  40.9 0.0 copy-done
  40.9 1.9 %collective-permute-start.6 = (bf16[32,2048]{1,0:T(8,128)(2,1)S(1)}, bf16[32,2048]{1,0:T(8,128)(2,1)S(1)}, u32[]{:S(2)}, u32[]{:S(2)}) collective-permute-start(bf16[32,2048]{1,0:T(8,128)(2,1)S(1)} %copy-done), channel_id=1, source_target_pairs={{15,16},{47,48},{63,64},{79,80},{111,112},{127,128},{143,144},{175... | collective-permute-start | bytes 393224 | tf_op jit(solution)/shard_map/ppermute | solution.py:232
  42.8 0.7 %collective-permute-start.5 = (bf16[32,2048]{1,0:T(8,128)(2,1)S(1)}, bf16[32,2048]{1,0:T(8,128)(2,1)S(1)}, u32[]{:S(2)}, u32[]{:S(2)}) collective-permute-start(bf16[32,2048]{1,0:T(8,128)(2,1)S(1)} %copy-done), channel_id=1, source_target_pairs={{1,2},{3,4},{5,6},{7,8},{9,10},{11,12},{13,14},{17,18},{19,20},{21... | collective-permute-start | bytes 393224 | tf_op jit(solution)/shard_map/ppermute | solution.py:231
  43.5 3.4 %collective-permute-start.4 = (bf16[32,2048]{1,0:T(8,128)(2,1)S(1)}, bf16[32,2048]{1,0:T(8,128)(2,1)S(1)}, u32[]{:S(2)}, u32[]{:S(2)}) collective-permute-start(bf16[32,2048]{1,0:T(8,128)(2,1)S(1)} %copy-done), channel_id=1, source_target_pairs={{0,1},{1,0},{4,5},{5,4},{6,7},{7,6},{10,11},{11,10},{14,15},{15,14... | collective-permute-start | bytes 393224 | tf_op jit(solution)/shard_map/ppermute | solution.py:230
  46.9 3.1 %collective-permute-done.3.partner = bf16[32,2048]{1,0:T(8,128)(2,1)S(1)} collective-permute-done((bf16[32,2048]{1,0:T(8,128)(2,1)S(1)}, bf16[32,2048]{1,0:T(8,128)(2,1)S(1)}, u32[]{:S(2)}, u32[]{:S(2)}) %collective-permute-start.3) | collective-permute-done | bytes 131104 | tf_op jit(solution)/shard_map/ppermute | solution.py:17
  50.0 0.5 level2.1.own
  50.5 7.1 %all-gather.1 = bf16[64,2048]{1,0:T(8,128)(2,1)S(1)} all-gather(bf16[32,2048]{1,0:T(8,128)(2,1)S(1)} %level2.1.own), channel_id=3, replica_groups={{0,128},{32,160},{64,192},{96,224},{256,384},{288,416},{320,448},{352,4..., dimensions={0}, use_global_device_ids=true | all-gather | bytes 393216 | tf_op jit(solution)/shard_map/all_gather | solution.py:22
  57.7 0.0 collective-permute-done.6.refs_5_
  57.7 0.0 collective-permute-done.5.refs_3_
  57.7 0.0 collective-permute-done.4.refs_1_
  57.7 2.1 %last.1 = (bf16[32,2048]{1,0:T(8,128)(2,1)}, bf16[32,2048]{1,0:T(8,128)(2,1)}) custom-call(s32[4,32]{1,0:T(4,128)S(4)} %get-tuple-element.13.pattern, s32[32]{0:T(128)S(4)} %get-tuple-element.14.order, s32[6,32]{1,0:T(8,128)S(4)} %get-tuple-element.15.neighbors, bf16[32,2048]{1,0:T(8,128)(2,1)S(1)} %level2.1.own, bf16[2,32,2048]{2,1,0:T(8,128)(2,1)S(1)} %bitcast.4, ...), custom_call_target="tpu_custom_call" | custom-call | flops 67108864 | bytes 5242880 | tf_op jit(solution)/shard_map/last/pallas_call | solution.py:173
Async XLA Ops:
  0.6 19.8 %collective-permute-start = (bf16[32,2048]{1,0:T(8,128)(2,1)}, bf16[32,2048]{1,0:T(8,128)(2,1)S(1)}, u32[]{:S(2)}, u32[]{:S(2)}) collective-permute-start(bf16[32,2048]{1,0:T(8,128)(2,1)} %refs_3_.1), channel_id=1, source_target_pairs={{0,16},{1,17},{2,18},{3,19},{4,20},{5,21},{6,22},{7,23},{8,24},{9,... | collective-permute-start | bytes 393224 | tf_op jit(solution)/shard_map/ppermute | solution.py:17
  16.4 11.7 %collective-permute-start.1 = (bf16[32,2048]{1,0:T(8,128)(2,1)}, bf16[32,2048]{1,0:T(8,128)(2,1)S(1)}, u32[]{:S(2)}, u32[]{:S(2)}) collective-permute-start(bf16[32,2048]{1,0:T(8,128)(2,1)} %refs_2_), channel_id=1, source_target_pairs={{31,32},{95,96},{159,160},{223,224},{287,288},{351,352},{415,416},... | collective-permute-start | bytes 393224 | tf_op jit(solution)/shard_map/ppermute | solution.py:207
  17.0 11.0 %collective-permute-start.2 = (bf16[32,2048]{1,0:T(8,128)(2,1)}, bf16[32,2048]{1,0:T(8,128)(2,1)S(1)}, u32[]{:S(2)}, u32[]{:S(2)}) collective-permute-start(bf16[32,2048]{1,0:T(8,128)(2,1)} %refs_2_), channel_id=1, source_target_pairs={{2,3},{3,2},{8,9},{9,8},{12,13},{13,12},{16,17},{17,16},{18,19},{1... | collective-permute-start | bytes 393224 | tf_op jit(solution)/shard_map/ppermute | solution.py:212
  20.4 20.5 %copy-start = (bf16[32,2048]{1,0:T(8,128)(2,1)S(1)}, bf16[32,2048]{1,0:T(8,128)(2,1)}, u32[]{:S(2)}) copy-start(bf16[32,2048]{1,0:T(8,128)(2,1)} %refs_2_) | copy-start | bytes 393220
  28.6 21.4 %collective-permute-start.3 = (bf16[32,2048]{1,0:T(8,128)(2,1)S(1)}, bf16[32,2048]{1,0:T(8,128)(2,1)S(1)}, u32[]{:S(2)}, u32[]{:S(2)}) collective-permute-start(bf16[32,2048]{1,0:T(8,128)(2,1)S(1)} %level1.1.own), channel_id=1, source_target_pairs={{0,8},{1,9},{2,10},{3,11},{4,12},{5,13},{6,14},{7,15},{8,0},{9,1},... | collective-permute-start | bytes 393224 | tf_op jit(solution)/shard_map/ppermute | solution.py:17
  40.9 16.7 %collective-permute-start.6 = (bf16[32,2048]{1,0:T(8,128)(2,1)S(1)}, bf16[32,2048]{1,0:T(8,128)(2,1)S(1)}, u32[]{:S(2)}, u32[]{:S(2)}) collective-permute-start(bf16[32,2048]{1,0:T(8,128)(2,1)S(1)} %copy-done), channel_id=1, source_target_pairs={{15,16},{47,48},{63,64},{79,80},{111,112},{127,128},{143,144},{175... | collective-permute-start | bytes 393224 | tf_op jit(solution)/shard_map/ppermute | solution.py:232
  42.8 14.8 %collective-permute-start.5 = (bf16[32,2048]{1,0:T(8,128)(2,1)S(1)}, bf16[32,2048]{1,0:T(8,128)(2,1)S(1)}, u32[]{:S(2)}, u32[]{:S(2)}) collective-permute-start(bf16[32,2048]{1,0:T(8,128)(2,1)S(1)} %copy-done), channel_id=1, source_target_pairs={{1,2},{3,4},{5,6},{7,8},{9,10},{11,12},{13,14},{17,18},{19,20},{21... | collective-permute-start | bytes 393224 | tf_op jit(solution)/shard_map/ppermute | solution.py:231
  43.5 14.1 %collective-permute-start.4 = (bf16[32,2048]{1,0:T(8,128)(2,1)S(1)}, bf16[32,2048]{1,0:T(8,128)(2,1)S(1)}, u32[]{:S(2)}, u32[]{:S(2)}) collective-permute-start(bf16[32,2048]{1,0:T(8,128)(2,1)S(1)} %copy-done), channel_id=1, source_target_pairs={{0,1},{1,0},{4,5},{5,4},{6,7},{7,6},{10,11},{11,10},{14,15},{15,14... | collective-permute-start | bytes 393224 | tf_op jit(solution)/shard_map/ppermute | solution.py:230
